TPU v7x, 32 devices: a whole 2x2x4 slice. The times are simulated.
32 devices in a mesh: dp: 8 (over y, x, core), seq: 4 (over z).
Axes of the slice: x: 2, y: 2, z: 4, core: 2. Of those that a mesh axis runs over, the one named last changes fastest.
Arguments:
- inputs: bfloat16 [16, 1024, 1024], P('dp', 'seq'), may hold values from -6 to 6
- out_grad: bfloat16 [16, 1024, 1024], P('dp', 'seq'), may hold values from -6 to 6
- norm_gain: float32 [2, 1024], replicated, may hold values from 0.3 to 2.4, as said below
- norm_bias: float32 [2, 1024], replicated, may hold values from -1.25 to 1.25
- proj_bias: float32 [4, 1024], replicated, may hold values from -1.25 to 1.25
- fc_bias: float32 [4096], replicated, may hold values from -1.25 to 1.25
- qkv_weight: bfloat16 [1024, 3072], P('dp'), may hold values from -0.1875 to 0.1875
- out_weight: bfloat16 [1024, 1024], P('dp'), may hold values from -2 to 2
- feed_input_weight: bfloat16 [1024, 4096], P('dp'), may hold values from -0.1875 to 0.1875
- proj_weight: bfloat16 [4096, 1024], P('dp'), may hold values from -0.09375 to 0.09375
- adapters: float32 [4, 4, 1024], replicated, may hold values from -0.1875 to 0.1875
- first_moment: float32 [4, 4, 1024], replicated, may hold values from -0.0048828125 to 0.0048828125
- second_moment: float32 [4, 4, 1024], replicated, may hold values from 6.103516e-08 to 2.4414064e-07
Outputs:
- mixed: bfloat16 [16, 1024, 1024], P('dp', 'seq')
- grad_in: bfloat16 [16, 1024, 1024], P('dp', 'seq')
- adapter_grad: float32 [4, 4, 1024], replicated
- grad_norm: float32 [], replicated
- new_adapters: float32 [4, 4, 1024], replicated
- new_first: float32 [4, 4, 1024], replicated
- new_second: float32 [4, 4, 1024], replicated
Inputs may be any that keep to these rules, and one draw needn't show every extreme that they name: `norm_gain`: positive gains of the two layer norms.
All inputs are finite; a program needn't handle non-finite values.
Results may differ from a plain program's by a relative error of at most 0.013.
Values may be sent and summed in bfloat16 or wider, within the bound.
No kernel may reach another device: no remote copies, remote signals or barrier semaphores. Data moves between devices by JAX's collectives and lax.ppermute only.
A program may use at most 192 MiB of HBM per device.

v0:
```python
import math

import jax
import jax.numpy as jnp
from jax import lax
from jax.sharding import PartitionSpec as P

HEAD_DIM = 64
ADAPTER_RANK = 4
STEP = 10


highest = lax.Precision.HIGHEST
adapter_alpha = 32.0
beta_one = 0.9
beta_two = 0.999
adam_eps = 1e-08
decay_rate = 0.01
learning_rate = 0.02
clip_bound = 1.0
norm_eps = 1e-05


def layer_norm(value, gain, shift):
    center = jnp.mean(value, axis=-1, keepdims=True)
    centered = value - center
    spread = jnp.mean(centered * centered, axis=-1, keepdims=True)
    return centered * lax.rsqrt(spread + norm_eps) * gain + shift


def dot_trans(left, right):
    return lax.dot_general(
        left, right, (((1,), (1,)), ((), ())), preferred_element_type=jnp.float32
    )


def dot_first(left, right):
    return lax.dot_general(
        left, right, (((0,), (0,)), ((), ())), precision=highest, preferred_element_type=jnp.float32
    )


def adam_update(grad, weight, first, second, norm):
    scale_factor = clip_bound / jnp.maximum(norm, clip_bound)
    clipped = grad * scale_factor
    new_first = beta_one * first + (1.0 - beta_one) * clipped
    new_second = beta_two * second + (1.0 - beta_two) * clipped * clipped
    first_hat = new_first / (1.0 - beta_one**STEP)
    second_hat = new_second / (1.0 - beta_two**STEP)
    new_weight = weight - learning_rate * (
        first_hat / (jnp.sqrt(second_hat) + adam_eps) + decay_rate * weight
    )
    return (clipped, new_weight, new_first, new_second)


def split_heads(packed):
    length = packed.shape[0]
    local_heads = packed.shape[-1] // HEAD_DIM
    query = packed[:, 0, 0].reshape(length, local_heads, HEAD_DIM)
    keys = packed[:, 1, 0].reshape(length, local_heads, HEAD_DIM)
    values = packed[:, 2, 0].reshape(length, local_heads, HEAD_DIM)
    return (query, keys, values)


def doc_forward(packed):
    length = packed.shape[0]
    local_width = packed.shape[-1]
    query, keys, values = split_heads(packed)
    local_heads = query.shape[1]
    span = min(512, length)
    blocks = length // span
    scale = 1.0 / math.sqrt(HEAD_DIM)
    starts = jnp.arange(blocks, dtype=jnp.int32) * span

    def visit(pieces):
        query_block, start = pieces
        scores = (
            jnp.einsum("qhd,khd->hqk", query_block, keys, preferred_element_type=jnp.float32)
            * scale
        )
        causal = (start + jnp.arange(span))[:, None] >= jnp.arange(length)[None, :]
        masked = jnp.where(causal[None], scores, -1e30)
        summit = jnp.max(masked, axis=-1, keepdims=True)
        expo = jnp.where(causal[None], jnp.exp(masked - summit), 0.0)
        totals = jnp.sum(expo, axis=-1, keepdims=True)
        weights = (expo / totals).astype(jnp.bfloat16)
        context = jnp.einsum(
            "hqk,khd->qhd", weights, values, preferred_element_type=jnp.float32
        ).astype(jnp.bfloat16)
        return (context, summit[..., 0] + jnp.log(totals[..., 0]))

    context, log_total = lax.map(
        visit, (query.reshape(blocks, span, local_heads, HEAD_DIM), starts)
    )
    return (context.reshape(length, 1, local_width), log_total)


def doc_backward(args):
    packed, grad_context, log_total = args
    length = packed.shape[0]
    local_width = packed.shape[-1]
    query, keys, values = split_heads(packed)
    local_heads = query.shape[1]
    output_gradient = grad_context[:, 0].reshape(length, local_heads, HEAD_DIM)
    span = min(512, length)
    blocks = length // span
    scale = 1.0 / math.sqrt(HEAD_DIM)
    starts = jnp.arange(blocks, dtype=jnp.int32) * span

    def visit(carry, pieces):
        grad_keys, grad_values = carry
        query_block, grad_block, total_block, start = pieces
        scores = (
            jnp.einsum("qhd,khd->hqk", query_block, keys, preferred_element_type=jnp.float32)
            * scale
        )
        causal = (start + jnp.arange(span))[:, None] >= jnp.arange(length)[None, :]
        masked = jnp.where(causal[None], scores, -1e30)
        probs = jnp.where(causal[None], jnp.exp(masked - total_block[:, :, None]), 0.0)
        weights = probs.astype(jnp.bfloat16)
        grad_probs = jnp.einsum(
            "qhd,khd->hqk", grad_block, values, preferred_element_type=jnp.float32
        )
        inner = jnp.sum(probs * grad_probs, axis=-1, keepdims=True)
        grad_scores = (probs * (grad_probs - inner)).astype(jnp.bfloat16)
        grad_query = (
            jnp.einsum("hqk,khd->qhd", grad_scores, keys, preferred_element_type=jnp.float32)
            * scale
        )
        grad_keys = (
            grad_keys
            + jnp.einsum(
                "hqk,qhd->khd", grad_scores, query_block, preferred_element_type=jnp.float32
            )
            * scale
        )
        grad_values = grad_values + jnp.einsum(
            "hqk,qhd->khd", weights, grad_block, preferred_element_type=jnp.float32
        )
        return ((grad_keys, grad_values), grad_query)

    empty = jnp.zeros((length, local_heads, HEAD_DIM), jnp.float32)
    pieces = (
        query.reshape(blocks, span, local_heads, HEAD_DIM),
        output_gradient.reshape(blocks, span, local_heads, HEAD_DIM),
        log_total,
        starts,
    )
    (grad_keys, grad_values), grad_query = lax.scan(visit, (empty, empty), pieces)
    joined = jnp.stack(
        [
            grad_query.reshape(length, local_width),
            grad_keys.reshape(length, local_width),
            grad_values.reshape(length, local_width),
        ],
        axis=1,
    )
    return joined.astype(jnp.bfloat16)[:, :, None, :]


def on_device(
    inputs,
    out_grad,
    norm_gain,
    norm_bias,
    proj_bias,
    fc_bias,
    qkv_weight,
    out_weight,
    feed_input_weight,
    proj_weight,
    adapters,
    first_moment,
    second_moment,
):
    docs, tokens, width = inputs.shape
    count = docs * tokens
    ranks = lax.axis_size("seq")
    scale_factor = adapter_alpha / ADAPTER_RANK

    def forward(stack):
        qkv_full, out_full, fc_full, proj_full = stack
        flat = inputs.reshape(count, width).astype(jnp.float32)
        normed, norm_one_back = jax.vjp(
            lambda value: layer_norm(value, norm_gain[0], norm_bias[0]), flat
        )
        base = jnp.dot(normed.astype(jnp.bfloat16), qkv_full, preferred_element_type=jnp.float32)
        down_q = jnp.dot(normed, adapters[0].T, precision=highest)
        down_v = jnp.dot(normed, adapters[2].T, precision=highest)
        query = (
            base[:, :width]
            + proj_bias[0]
            + scale_factor * jnp.dot(down_q, adapters[1], precision=highest)
        )
        keys = base[:, width : 2 * width]
        values = (
            base[:, 2 * width :]
            + proj_bias[1]
            + scale_factor * jnp.dot(down_v, adapters[3], precision=highest)
        )
        joined = (
            jnp.concatenate([query, keys, values], axis=1)
            .astype(jnp.bfloat16)
            .reshape(docs, tokens, 3, ranks, width // ranks)
        )
        spread = lax.all_to_all(joined, "seq", split_axis=3, concat_axis=1, tiled=True)
        context, log_total = lax.map(doc_forward, spread)
        context = lax.all_to_all(context, "seq", split_axis=1, concat_axis=2, tiled=True).reshape(
            count, width
        )
        middle = (
            flat + jnp.dot(context, out_full, preferred_element_type=jnp.float32) + proj_bias[2]
        )
        normed_two, norm_two_back = jax.vjp(
            lambda value: layer_norm(value, norm_gain[1], norm_bias[1]), middle
        )
        hidden = (
            jnp.dot(normed_two.astype(jnp.bfloat16), fc_full, preferred_element_type=jnp.float32)
            + fc_bias
        )
        active, gelu_back = jax.vjp(lambda value: jax.nn.gelu(value, approximate=True), hidden)
        result = (
            middle
            + jnp.dot(active.astype(jnp.bfloat16), proj_full, preferred_element_type=jnp.float32)
            + proj_bias[3]
        )
        return (
            result,
            (normed, down_q, down_v, norm_one_back, spread, log_total, norm_two_back, gelu_back),
        )

    stack = (
        lax.all_gather(qkv_weight, "dp", axis=0, tiled=True),
        lax.all_gather(out_weight, "dp", axis=0, tiled=True),
        lax.all_gather(feed_input_weight, "dp", axis=0, tiled=True),
        lax.all_gather(proj_weight, "dp", axis=0, tiled=True),
    )
    result, kept = forward(stack)
    fenced = lax.optimization_barrier((stack, result))
    stack = fenced[0]
    again, kept = forward(stack)
    qkv_full, out_full, fc_full, proj_full = stack
    normed, down_q, down_v, norm_one_back, spread, log_total, norm_two_back, gelu_back = kept
    cotangent = out_grad.reshape(count, width)
    grad_active = dot_trans(cotangent, proj_full)
    grad_hidden = gelu_back(grad_active)[0].astype(jnp.bfloat16)
    grad_normed_two = dot_trans(grad_hidden, fc_full)
    grad_middle = cotangent.astype(jnp.float32) + norm_two_back(grad_normed_two)[0]
    grad_context = dot_trans(grad_middle.astype(jnp.bfloat16), out_full).astype(jnp.bfloat16)
    grad_context = grad_context.reshape(docs, tokens, ranks, width // ranks)
    grad_context = lax.all_to_all(grad_context, "seq", split_axis=2, concat_axis=1, tiled=True)
    grad_joined = lax.map(doc_backward, (spread, grad_context, log_total))
    grad_joined = lax.all_to_all(
        grad_joined, "seq", split_axis=1, concat_axis=3, tiled=True
    ).reshape(count, 3 * width)
    grad_normed = dot_trans(grad_joined, qkv_full)
    grad_query = grad_joined[:, :width].astype(jnp.float32)
    grad_value = grad_joined[:, 2 * width :].astype(jnp.float32)
    tilt_q = scale_factor * jnp.dot(grad_query, adapters[1].T, precision=highest)
    value_adapter_up = scale_factor * jnp.dot(grad_value, adapters[3].T, precision=highest)
    grad_normed = (
        grad_normed
        + jnp.dot(tilt_q, adapters[0], precision=highest)
        + jnp.dot(value_adapter_up, adapters[2], precision=highest)
    )
    grad_input = (
        (grad_middle + norm_one_back(grad_normed)[0])
        .astype(jnp.bfloat16)
        .reshape(docs, tokens, width)
    )
    partial_terms = jnp.stack(
        [
            dot_first(tilt_q, normed),
            scale_factor * dot_first(down_q, grad_query),
            dot_first(value_adapter_up, normed),
            scale_factor * dot_first(down_v, grad_value),
        ]
    )
    total = lax.psum(partial_terms, ("dp", "seq"))
    grad_norm = jnp.sqrt(jnp.sum(total * total))
    clipped, new_weight, new_first, new_second = adam_update(
        total, adapters, first_moment, second_moment, grad_norm
    )
    mixed = result.astype(jnp.bfloat16).reshape(docs, tokens, width)
    return (mixed, grad_input, clipped, grad_norm, new_weight, new_first, new_second)


def solution(mesh):
    return jax.shard_map(
        on_device,
        mesh=mesh,
        in_specs=(
            P("dp", "seq", None),
            P("dp", "seq", None),
            P(),
            P(),
            P(),
            P(),
            P("dp", None),
            P("dp", None),
            P("dp", None),
            P("dp", None),
            P(),
            P(),
            P(),
        ),
        out_specs=(P("dp", "seq", None), P("dp", "seq", None), P(), P(), P(), P(), P()),
        check_vma=False,
    )
```

profile of v0, /device:TPU:9, one launch (start us, length us, event | category | flops | bytes accessed | tf_op | source)
XLA Modules:
  0.0 874.1 jit_solution(17009946476179839401)
XLA Ops:
  20.4 36.8 %all-gather.5.cloned.1.call-done = bf16[1024,3072]{1,0:T(8,128)(2,1)} async-done(((bf16[128,3072]{1,0:T(8,128)(2,1)}), bf16[1024,3072]{1,0:T(8,128)(2,1)}) %all-gather.5.cloned.1.call-update) | async-done | bytes 6291472 | tf_op jit(solution)/shard_map/all_gather | solution.py:233
  57.3 5.7 fusion.124
  65.7 21.3 %all-gather.7.cloned.1.call-done = bf16[1024,1024]{1,0:T(8,128)(2,1)} async-done(((bf16[128,1024]{1,0:T(8,128)(2,1)}), bf16[1024,1024]{1,0:T(8,128)(2,1)}) %all-gather.7.cloned.1.call-update) | async-done | bytes 2097168 | tf_op jit(solution)/shard_map/all_gather | solution.py:234
  87.1 56.3 %all-gather.9.cloned.1.call-done = bf16[1024,4096]{1,0:T(8,128)(2,1)} async-done(((bf16[128,4096]{1,0:T(8,128)(2,1)}), bf16[1024,4096]{1,0:T(8,128)(2,1)}) %all-gather.9.cloned.1.call-update) | async-done | bytes 8388624 | tf_op jit(solution)/shard_map/all_gather | solution.py:235
  143.4 56.2 %all-gather.11.cloned.1.call-done = bf16[4096,1024]{1,0:T(8,128)(2,1)} async-done(((bf16[512,1024]{1,0:T(8,128)(2,1)}), bf16[4096,1024]{1,0:T(8,128)(2,1)}) %all-gather.11.cloned.1.call-update) | async-done | bytes 8388624 | tf_op jit(solution)/shard_map/all_gather | solution.py:236
  226.9 6.7 convert_element_type.92
  237.6 56.5 %all-to-all-done.2 = bf16[2,256,3,4,256]{4,1,2,0,3:T(8,128)(2,1)S(1)} async-done(((bf16[2,256,3,4,256]{4,1,2,0,3:T(8,128)(2,1)}), bf16[2,256,3,4,256]{4,1,2,0,3:T(8,128)(2,1)S(1)}, u32[]{:S(2)}, u32[]{:S(2)}) %all-to-all-start.2) | async-done | bytes 3145760 | tf_op jit(solution)/shard_map/all_to_all | solution.py:206
  294.1 7.9 all-to-all-start
  308.2 58.6 %while.72 = (s32[]{:T(128)}, bf16[2,1024,1,256]{1,3,2,0:T(8,128)(2,1)}, f32[2,2,4,512]{3,2,1,0:T(4,128)S(1)}, bf16[2,1024,3,1,256]{1,4,2,3,0:T(8,128)(2,1)S(1)}, s32[]{:T(128)}, /*index=5*/s32[]{:T(128)}, s32[]{:T(128)}) while((s32[]{:T(128)}, bf16[2,1024,1,256]{1,3,2,0:T(8,128)(2,1)}, f32[2,2,4,512]{3,2,1,0:T(4,128)S(1)}, ...), condition=%wide.region_15.16_spmd, body=%wide.region_10.15_spmd.sunk | while | flops 566884864 | bytes 65638752 | solution.py:207
  310.6 20.3 %while.76 = (s32[]{:T(128)}, bf16[2,512,4,64]{1,3,2,0:T(8,128)(2,1)}, f32[2,4,512]{2,1,0:T(4,128)S(1)}, s32[2]{0:T(128)S(1)}, bf16[2,512,4,64]{1,3,2,0:T(8,128)(...) while((s32[]{:T(128)}, ...), condition=%wide.region_14.14_spmd, body=%wide.region_11.13_spmd.sunk | while | flops 566884864 | bytes 28905592 | solution.py:92
  339.9 20.3 %while.76 = (s32[]{:T(128)}, bf16[2,512,4,64]{1,3,2,0:T(8,128)(2,1)}, f32[2,4,512]{2,1,0:T(4,128)S(1)}, s32[2]{0:T(128)S(1)}, bf16[2,512,4,64]{1,3,2,0:T(8,128)(...) while((s32[]{:T(128)}, ...), condition=%wide.region_14.14_spmd, body=%wide.region_11.13_spmd.sunk | while | flops 566884864 | bytes 28905592 | solution.py:92
  370.7 6.2 all-to-all-start.3
  376.8 11.5 %fusion.170 = f32[4096,512]{0,1:T(8,128)} fusion(bf16[4096,1024]{1,0:T(8,128)(2,1)} %all-gather.11.cloned.1.call-done, bf16[512,1024]{1,0:T(8,128)(2,1)} %bitcast.355), kind=kOutput, calls=%fused_computation.243 | convolution fusion | flops 4294967296 | bytes 17825792 | tf_op jit(solution)/shard_map/dot_general | solution.py:32
  392.1 5.6 all-to-all-done.3
  402.1 21.3 %multiply_reduce_fusion.1 = (f32[512]{0:T(512)S(1)}, f32[512,1024]{1,0:T(8,128)}) fusion(f32[512,1024]{1,0:T(8,128)S(1)} %get-tuple-element.481, f32[512]{0:T(512)S(1)} %broadcast_multiply_fusion.1, f32[1024]{0:T(1024)S(1)} %bitcast.373, bf16[1024,4096]{1,0:T(8,128)(2,1)} %all-gather.9.cloned.1.call-done, f32[4096,512]{0,1:T(8,128)} %fusion.170, ...), kind=kOutput, calls=%fused_computation.150 | convolution fusion | flops 8638693376 | bytes 21002240 | tf_op jit(solution)/shard_map/dot_general | solution.py:32
  430.5 8.2 all-to-all-start.4
  439.8 72.3 %while.70 = (s32[]{:T(128)}, bf16[2,1024,1,256]{1,3,2,0:T(8,128)(2,1)}, bf16[2,1024,3,1,256]{4,1,2,0,3:T(8,128)(2,1)}, s32[]{:T(128)}, s32[]{:T(128)}, /*index=5*/s32[]{:T(128)}) while((s32[]{:T(128)}, bf16[2,1024,1,256]{1,3,2,0:T(8,128)(2,1)}, bf16[2,1024,3,1,256]{4,1,2,0,3:T(8,128)(2,1)}, s32[]{:T(128)}, s32[]{:T(128)}, ...), condition=%wide.region_7.8_spmd, body=%wide.region_2.7_spmd.sunk | while | flops 556402176 | bytes 61362524 | solution.py:207
  445.6 28.4 %while.75 = (s32[]{:T(128)}, bf16[2,512,4,64]{1,3,2,0:T(8,128)(2,1)S(1)}, s32[2]{0:T(128)S(1)}, bf16[2,512,4,64]{1,3,2,0:T(8,128)(2,1)S(1)}, bf16[1024,4,64]{0,2...) while((s32[]{:T(128)}, bf16[2,512,4,64]{1,3,2,0:T(8,128)(2,1)S(1)}, s32[2]{0:T(128)S(1)}, ...), condition=%wide.region_6.6_spmd, body=%wide.region_3.5_spmd.sunk | while | flops 556402176 | bytes 38293640 | solution.py:92
  448.6 6.4 fusion.265
  462.8 6.4 fusion.265
  481.7 28.4 %while.75 = (s32[]{:T(128)}, bf16[2,512,4,64]{1,3,2,0:T(8,128)(2,1)S(1)}, s32[2]{0:T(128)S(1)}, bf16[2,512,4,64]{1,3,2,0:T(8,128)(2,1)S(1)}, bf16[1024,4,64]{0,2...) while((s32[]{:T(128)}, bf16[2,512,4,64]{1,3,2,0:T(8,128)(2,1)S(1)}, s32[2]{0:T(128)S(1)}, ...), condition=%wide.region_6.6_spmd, body=%wide.region_3.5_spmd.sunk | while | flops 556402176 | bytes 38293640 | solution.py:92
  484.7 6.4 fusion.265
  498.9 6.4 fusion.265
  523.0 107.5 %while.74 = (s32[]{:T(128)}, bf16[2,1024,3,1,256]{1,4,3,2,0:T(8,128)(2,1)}, bf16[2,1024,3,1,256]{1,4,2,3,0:T(8,128)(2,1)}, bf16[2,1024,1,256]{3,1,0,2:T(8,128)(2...) while((s32[]{:T(128)}, ...), condition=%wide.region_24.25_spmd, body=%wide.region_20.24_spmd.sunk | while | flops 1370356224 | bytes 187773584 | solution.py:252
  532.0 41.5 %while.77 = (s32[]{:T(128)}, f32[1024,4,64]{0,2,1:T(8,128)S(1)}, f32[1024,4,64]{0,2,1:T(8,128)S(1)}, bf16[2,512,4,64]{1,3,2,0:T(8,128)(2,1)}, bf16[2,512,4,64]{1...) while((s32[]{:T(128)}, f32[1024,4,64]{0,2,1:T(8,128)S(1)}, ...), condition=%wide.region_23.23_spmd.clone, body=%wide.region_21.22_spmd.clone.sunk | while | flops 1365113344 | bytes 165720464 | solution.py:149
  585.7 41.5 %while.77 = (s32[]{:T(128)}, f32[1024,4,64]{0,2,1:T(8,128)S(1)}, f32[1024,4,64]{0,2,1:T(8,128)S(1)}, bf16[2,512,4,64]{1,3,2,0:T(8,128)(2,1)}, bf16[2,512,4,64]{1...) while((s32[]{:T(128)}, f32[1024,4,64]{0,2,1:T(8,128)S(1)}, ...), condition=%wide.region_23.23_spmd.clone, body=%wide.region_21.22_spmd.clone.sunk | while | flops 1365113344 | bytes 165720464 | solution.py:149
  630.5 8.8 %copy.116 = bf16[2,1024,3,1,256]{4,0,3,2,1:T(2,128)(2,1)} copy(bf16[2,1024,3,1,256]{1,4,3,2,0:T(8,128)(2,1)} %get-tuple-element.209) | data formatting | bytes 6291456 | tf_op jit(solution)/shard_map/while | solution.py:252
  648.6 16.3 %fusion.100 = bf16[512,1024]{1,0:T(8,128)(2,1)} fusion(f32[512,1024]{1,0:T(8,128)S(1)} %get-tuple-element.479, f32[1024]{0:T(1024)S(1)} %bitcast.378, bf16[4096,1024]{1,0:T(8,128)(2,1)} %all-gather.11.cloned.1.call-done, bf16[1024,4096]{1,0:T(8,128)(2,1)} %all-gather.9.cloned.1.call-done, f32[4096]{0:T(1024)S(1)} %copy-done.59, f32[1024]{0:T(1024)S(1)} %bitcast.377, ...), kind=kOutput, calls=%fused_computation.154 | convolution fusion | flops 8615100416 | bytes 19955712 | tf_op jit(solution)/shard_map/dot_general | solution.py:224
  664.9 44.3 %all-to-all-done.5 = bf16[2,1024,3,1,256]{4,0,3,2,1:T(2,128)(2,1)} async-done(((bf16[2,1024,3,1,256]{4,0,3,2,1:T(2,128)(2,1)}), bf16[2,1024,3,1,256]{4,0,3,2,1:T(2,128)(2,1)}, u32[]{:S(2)}, u32[]{:S(2)}) %all-to-all-start.5) | async-done | bytes 3145760 | tf_op jit(solution)/shard_map/all_to_all | solution.py:253
  715.7 6.5 reshape.324
  724.4 6.7 fusion.171
  744.8 117.6 %all-reduce.2.cloned.1.call-done = f32[4,4,1024]{2,1,0:T(4,128)} async-done(((f32[4,4,1024]{2,1,0:T(4,128)}), f32[4,4,1024]{2,1,0:T(4,128)}) %all-reduce.2.cloned.1.call-update) | async-done | bytes 65552 | tf_op jit(solution)/shard_map/psum | solution.py:279
  (434 shorter events, 330.9 us)
Async XLA Ops:
  7.2 50.0 %all-gather.5.cloned.1.call-start = ((), (), s32[]{:S(2)}) async-start(), calls=%async_computation.6 | async-start | bytes 7077888 | tf_op jit(solution)/shard_map/all_gather | solution.py:233
  7.9 79.1 %all-gather.7.cloned.1.call-start = ((), (), s32[]{:S(2)}) async-start(), calls=%async_computation.7 | async-start | bytes 2359296 | tf_op jit(solution)/shard_map/all_gather | solution.py:234
  8.7 134.7 %all-gather.9.cloned.1.call-start = ((), (), s32[]{:S(2)}) async-start(), calls=%async_computation.8 | async-start | bytes 9437184 | tf_op jit(solution)/shard_map/all_gather | solution.py:235
  9.4 190.1 %all-gather.11.cloned.1.call-start = ((), (), s32[]{:S(2)}) async-start(), calls=%async_computation.9 | async-start | bytes 9437184 | tf_op jit(solution)/shard_map/all_gather | solution.py:236
  10.7 9.3 %copy-start.39 = (f32[512]{0:T(512)}, f32[512]{0:T(512)S(1)}, u32[]{:S(2)}) copy-start(f32[512]{0:T(512)S(1)} %rsqrt.32) | copy-start | bytes 6148
  10.7 9.3 %copy-start.37 = (f32[1,2,2,128]{3,1,2,0:T(2,128)}, f32[1,2,2,128]{3,1,2,0:T(2,128)S(1)}, u32[]{:S(2)}) copy-start(f32[1,2,2,128]{3,1,2,0:T(2,128)S(1)} %copy.124) | copy-start | bytes 6148
  11.9 8.1 copy-start.33
  16.7 188.5 %copy-start.29 = (f32[512,4]{0,1:T(4,128)}, f32[512,4]{0,1:T(4,128)S(1)}, u32[]{:S(2)}) copy-start(f32[512,4]{0,1:T(4,128)S(1)} %fusion.138) | copy-start | bytes 24580
  20.4 179.1 %copy-start.12 = (f32[512,1024]{1,0:T(8,128)}, f32[512,1024]{1,0:T(8,128)S(1)}, u32[]{:S(2)}) copy-start(f32[512,1024]{1,0:T(8,128)S(1)} %fusion.96) | copy-start | bytes 6291460
  222.3 71.8 %all-to-all-start.2 = ((bf16[2,256,3,4,256]{4,1,2,0,3:T(8,128)(2,1)}), bf16[2,256,3,4,256]{4,1,2,0,3:T(8,128)(2,1)S(1)}, u32[]{:S(2)}, u32[]{:S(2)}) async-start(bf16[2,256,3,4,256]{4,1,2,0,3:T(8,128)(2,1)} %copy.106), calls=%async_computation.2 | async-start | bytes 6291456 | tf_op jit(solution)/shard_map/all_to_all | solution.py:206
  294.1 76.6 %all-to-all-start = ((bf16[2,256,3,4,256]{4,1,2,0,3:T(8,128)(2,1)}), bf16[2,256,3,4,256]{4,1,2,0,3:T(8,128)(2,1)}, u32[]{:S(2)}, u32[]{:S(2)}) async-start(bf16[2,256,3,4,256]{4,1,2,0,3:T(8,128)(2,1)} %copy.99), calls=%async_computation | async-start | bytes 6291456 | tf_op jit(solution)/shard_map/all_to_all | solution.py:206
  330.9 6.6 copy-start.7
  360.2 6.6 copy-start.7
  366.8 21.5 %copy-start.8 = (bf16[2,1024,3,1,256]{1,4,2,3,0:T(8,128)(2,1)}, bf16[2,1024,3,1,256]{1,4,2,3,0:T(8,128)(2,1)S(1)}, u32[]{:S(2)}) copy-start(bf16[2,1024,3,1,256]{1,4,2,3,0:T(8,128)(2,1)S(1)} %get-tuple-element.947) | copy-start | bytes 9437188
  366.8 21.5 %copy-start.27 = (f32[2,2,4,512]{3,2,1,0:T(4,128)}, f32[2,2,4,512]{3,2,1,0:T(4,128)S(1)}, u32[]{:S(2)}) copy-start(f32[2,2,4,512]{3,2,1,0:T(4,128)S(1)} %get-tuple-element.919) | copy-start | bytes 98308
  370.7 27.1 %all-to-all-start.3 = ((bf16[2,1024,1,256]{3,0,2,1:T(2,128)(2,1)}), bf16[2,1024,1,256]{3,0,2,1:T(2,128)(2,1)}, u32[]{:S(2)}, u32[]{:S(2)}) async-start(bf16[2,1024,1,256]{3,0,2,1:T(2,128)(2,1)} %copy.109), calls=%async_computation.3 | async-start | bytes 2097152 | tf_op jit(solution)/shard_map/all_to_all | solution.py:208
  392.1 8.2 copy-start.10
  392.1 8.2 copy-start.53
  430.5 85.3 %all-to-all-start.4 = ((bf16[2,256,4,256]{3,1,0,2:T(8,128)(2,1)}), bf16[2,256,4,256]{3,1,0,2:T(8,128)(2,1)}, u32[]{:S(2)}, u32[]{:S(2)}) async-start(bf16[2,256,4,256]{3,1,0,2:T(8,128)(2,1)} %copy.112), calls=%async_computation.4 | async-start | bytes 2097152 | tf_op jit(solution)/shard_map/all_to_all | solution.py:251
  445.6 29.4 %copy-start.21 = (bf16[2,1024,1,256]{1,3,2,0:T(8,128)(2,1)S(1)}, bf16[2,1024,1,256]{1,3,2,0:T(8,128)(2,1)}, u32[]{:S(2)}) copy-start(bf16[2,1024,1,256]{1,3,2,0:T(8,128)(2,1)} %get-tuple-element.883) | copy-start | bytes 3145732 | tf_op jit(solution)/shard_map/while
  448.6 6.4 copy-start.18
  481.7 29.4 %copy-start.21 = (bf16[2,1024,1,256]{1,3,2,0:T(8,128)(2,1)S(1)}, bf16[2,1024,1,256]{1,3,2,0:T(8,128)(2,1)}, u32[]{:S(2)}) copy-start(bf16[2,1024,1,256]{1,3,2,0:T(8,128)(2,1)} %get-tuple-element.883) | copy-start | bytes 3145732 | tf_op jit(solution)/shard_map/while
  512.1 10.9 %copy-start.28 = (f32[2,2,4,512]{3,2,1,0:T(4,128)S(1)}, f32[2,2,4,512]{3,2,1,0:T(4,128)}, u32[]{:S(2)}) copy-start(f32[2,2,4,512]{3,2,1,0:T(4,128)} %copy-done.27) | copy-start | bytes 98308
  515.8 123.5 %all-to-all-start.1 = ((bf16[2,1024,1,256]{3,0,2,1:T(2,128)(2,1)}), bf16[2,1024,1,256]{3,0,2,1:T(2,128)(2,1)}, u32[]{:S(2)}, u32[]{:S(2)}) async-start(bf16[2,1024,1,256]{3,0,2,1:T(2,128)(2,1)} %copy.102), calls=%async_computation.1 | async-start | bytes 2097152 | tf_op jit(solution)/shard_map/all_to_all | solution.py:208
  639.3 69.9 %all-to-all-start.5 = ((bf16[2,1024,3,1,256]{4,0,3,2,1:T(2,128)(2,1)}), bf16[2,1024,3,1,256]{4,0,3,2,1:T(2,128)(2,1)}, u32[]{:S(2)}, u32[]{:S(2)}) async-start(bf16[2,1024,3,1,256]{4,0,3,2,1:T(2,128)(2,1)} %copy.116), calls=%async_computation.5 | async-start | bytes 6291456 | tf_op jit(solution)/shard_map/all_to_all | solution.py:253
  643.9 218.4 %all-reduce.2.cloned.1.call-start = ((), (), s32[]{:S(2)}) async-start(), calls=%async_computation.10 | async-start | bytes 131072 | tf_op jit(solution)/shard_map/psum | solution.py:279
  715.7 6.5 copy-start.26
  724.3 6.7 copy-start.14
  724.3 7.6 copy-start.32
  724.4 8.2 copy-start.30
  741.0 123.5 %copy-start.35 = (f32[4,4,1024]{2,1,0:T(4,128)S(1)}, f32[4,4,1024]{2,1,0:T(4,128)}, u32[]{:S(2)}) copy-start(f32[4,4,1024]{2,1,0:T(4,128)} %param.36) | copy-start | bytes 196612
  741.0 123.5 %copy-start.36 = (f32[4,4,1024]{2,1,0:T(4,128)S(1)}, f32[4,4,1024]{2,1,0:T(4,128)}, u32[]{:S(2)}) copy-start(f32[4,4,1024]{2,1,0:T(4,128)} %param.37) | copy-start | bytes 196612
  (71 other events, 201.3 us)
Sparse Core Ops, SparseCore 0:
  9.9 47.2 all-gather.4
  59.1 27.8 all-gather.6
  89.0 54.3 all-gather.8
  145.1 54.3 all-gather.10
  741.1 121.1 all-reduce.1
where the time goes:
time: 884 us; the launch traced here: 874 us
  waiting for transfers between devices  397 us (45%)
  matrix products  184 us (21%)
  local copies, waits for them, and re-layouts  161 us (18%)
  other arithmetic  78.2 us (9%)
  starting transfers between devices  36.7 us (4%)
  between operations  16.6 us (2%)
    psum x1, waiting for transfers between devices, on_device(): total = lax.psum(partial_terms, ('dp', 'seq'))  118 us
    all_to_all x2, waiting for transfers between devices, forward(): lax.all_to_all(joined, 'seq', split_axis=3, concat_axis=1, tiled=True)  56.5 us
    all_gather x1, waiting for transfers between devices, on_device(): lax.all_gather(feed_input_weight, 'dp', axis=0, tiled=True)  56.3 us
    all_gather x1, waiting for transfers between devices, on_device(): lax.all_gather(proj_weight, 'dp', axis=0, tiled=True)  56.2 us
    all_to_all x1, waiting for transfers between devices, on_device(): lax.all_to_all(grad_joined, 'seq', split_axis=1, concat_axis=3, tiled=True)  44.3 us
    dot_general x4, matrix products, dot_trans(): lax.dot_general(left, right, (((1,), (1,)), ((), ())), preferred_element_...  40.8 us
    all_gather x1, waiting for transfers between devices, on_device(): lax.all_gather(qkv_weight, 'dp', axis=0, tiled=True)  36.8 us
    dot_general x8, matrix products, visit(): jnp.einsum('hqk,khd->qhd', weights, values, preferred_element_type=jnp.fl...  35.2 us
  transfers between devices with their start and end apart: 11, of which 8 were waited for; matrix products, arithmetic and copies ran while one was open for 34% of the time, Pallas kernels for 0%

commit v1 on v0

--- a/solution.py
+++ b/solution.py
@@ -1,8 +1,12 @@
+import functools
 import math
 
 import jax
 import jax.numpy as jnp
 from jax import lax
+from jax.experimental import pallas as pl
+from jax.experimental.pallas import tpu as pltpu
+from jax.sharding import Mesh
 from jax.sharding import PartitionSpec as P
 
 HEAD_DIM = 64
@@ -285,25 +289,755 @@
     return (mixed, grad_input, clipped, grad_norm, new_weight, new_first, new_second)
 
 
+HALF = 512
+BLOCK = 256
+SMEM = pl.BlockSpec(memory_space=pltpu.SMEM)
+VMEM = pl.BlockSpec(memory_space=pltpu.VMEM)
+HBM = pl.BlockSpec(memory_space=pl.ANY)
+f32 = jnp.float32
+bf16 = jnp.bfloat16
+SWAP = ((0, 1), (1, 0))
+GELU_A = math.sqrt(2.0 / math.pi)
+GELU_B = 0.044715
+
+
+def nn(left, right):
+    return lax.dot_general(left, right, (((1,), (0,)), ((), ())), preferred_element_type=f32)
+
+
+def nt(left, right):
+    return lax.dot_general(left, right, (((1,), (1,)), ((), ())), preferred_element_type=f32)
+
+
+def tn(left, right):
+    return lax.dot_general(left, right, (((0,), (0,)), ((), ())), preferred_element_type=f32)
+
+
+def shape(*dims, dtype=bf16):
+    return jax.ShapeDtypeStruct(dims, dtype)
+
+
+def params(mib):
+    return pltpu.CompilerParams(vmem_limit_bytes=mib * 2**20)
+
+
+def rows(index, size):
+    return pl.ds(pl.multiple_of(index * size, size), size)
+
+
+def parity(z, k):
+    return lax.rem(z + k, 2)
+
+
+class Copies:
+    def __init__(self, sems):
+        self.sems = sems
+        self.count = 0
+
+    def start(self, source, target):
+        copy = pltpu.make_async_copy(source, target, self.sems.at[self.count])
+        self.count += 1
+        copy.start()
+        return copy
+
+
+def wait_all(copies):
+    for copy in copies:
+        copy.wait()
+
+
+def center_scale(x):
+    center = jnp.mean(x, axis=-1, keepdims=True)
+    centered = x - center
+    spread = jnp.mean(centered * centered, axis=-1, keepdims=True)
+    inverse = lax.rsqrt(spread + norm_eps)
+    return centered * inverse, inverse
+
+
+def norm_back(hat, inverse, grad):
+    first = jnp.mean(grad, axis=-1, keepdims=True)
+    second = jnp.mean(grad * hat, axis=-1, keepdims=True)
+    return inverse * (grad - first - hat * second)
+
+
+def qkv_kernel(
+    ids, m0, m1, o0, o1, w0, w1, w2, w3t, w3b, gain, shift, down_w, up_w, bias,
+    q_out, k_out, v_out, n_out, down_out, w_out, xs, ws, sems,
+):
+    core, z, chip = ids[0], ids[1], ids[2]
+    go = Copies(sems)
+    arrive = [
+        go.start(ref, xs.at[rows(2 * side + parity(z, k), BLOCK)])
+        for side, pair in ((core, (m0, m1)), (1 - core, (o0, o1)))
+        for k, ref in enumerate(pair)
+    ]
+    weights = [
+        go.start(ref, ws.at[rows(chip ^ r, BLOCK)]) for r, ref in enumerate((w0, w1, w2))
+    ]
+    weights.append(go.start(w3t, ws.at[rows(2 * (chip ^ 3), BLOCK // 2)]))
+    weights.append(go.start(w3b, ws.at[rows(2 * (chip ^ 3) + 1, BLOCK // 2)]))
+    wait_all(arrive)
+
+    @pl.loop(0, 4)
+    def _(i):
+        at = rows(i, BLOCK)
+        hat, _ = center_scale(xs[at].astype(f32))
+        n_out[at] = (hat * gain[...] + shift[...]).astype(bf16)
+
+    wait_all(weights)
+    keep = go.start(ws, w_out)
+
+    @pl.loop(0, 4)
+    def _(i):
+        at = rows(i, BLOCK)
+        n = n_out[at]
+        down = nt(n, down_w[...]).astype(bf16)
+        down_out[at] = down
+        for part, out in enumerate((q_out, k_out, v_out)):
+            cols = slice(part * HALF, (part + 1) * HALF)
+            value = nn(n, ws[:, cols]) + bias[:, cols]
+            if part != 1:
+                value += nn(down, up_w[:, cols])
+            value = value.astype(bf16)
+            if part == 0:
+                value = value * jnp.asarray(0.125, bf16)
+            out[at] = value
+
+    keep.wait()
+
+
+def call_qkv(ids, x_own, x_other, pieces, gain, shift, down_w, up_w, bias):
+    return pl.pallas_call(
+        qkv_kernel,
+        out_shape=(
+            shape(1024, HALF),
+            shape(1024, HALF),
+            shape(1024, HALF),
+            shape(1024, 1024),
+            shape(1024, 128),
+            shape(1024, 1536),
+        ),
+        in_specs=[SMEM] + [HBM] * 9 + [VMEM] * 5,
+        out_specs=(VMEM,) * 5 + (HBM,),
+        scratch_shapes=[
+            pltpu.VMEM((1024, 1024), bf16),
+            pltpu.VMEM((1024, 1536), bf16),
+            pltpu.SemaphoreType.DMA((10,)),
+        ],
+        compiler_params=params(40),
+        name="qkv",
+    )(ids, *x_own, *x_other, *pieces, gain, shift, down_w, up_w, bias)
+
+
+def low_half(value):
+    return lax.broadcasted_iota(jnp.int32, value.shape, 1) < 64
+
+
+def forward_kernel(ids, q, k, v, ctx, stat, send):
+    core = ids[0]
+    keys = k[...]
+    values = v[...]
+    low = low_half(values)
+    one = jnp.ones_like(values)
+    values_ab = (jnp.where(low, values, one), jnp.where(low, one, values))
+    for i in range(4):
+        ext = (i + 1) * BLOCK
+        query = q[i * BLOCK : ext]
+        mine = low_half(query)
+        zero = jnp.zeros_like(query)
+        heads, tops = [], []
+        for a in range(2):
+            part = jnp.where(mine, query, zero) if a == 0 else jnp.where(mine, zero, query)
+            scores = nt(part, keys[:ext])
+            last = scores[:, i * BLOCK :]
+            r = lax.broadcasted_iota(jnp.int32, last.shape, 0)
+            s = lax.broadcasted_iota(jnp.int32, last.shape, 1)
+            last = jnp.where(r >= s, last, -1e30)
+            scores = jnp.concatenate([scores[:, : i * BLOCK], last], axis=1) if i else last
+            top = jnp.max(scores, axis=1, keepdims=True)
+            expo = jnp.exp(scores - top).astype(bf16)
+            heads.append(nn(expo, values_ab[a][:ext]))
+            tops.append(top)
+        wide = low_half(heads[0])
+        sums = jnp.where(wide, heads[1], heads[0])
+        sums = pltpu.roll(sums, 64, 1)
+        ctx[i * BLOCK : ext] = (jnp.where(wide, heads[0], heads[1]) / sums).astype(bf16)
+        total = jnp.where(wide, tops[0], tops[1]) + jnp.log(sums)
+        total = jnp.transpose(total)
+        stat[0, :, i * BLOCK : ext] = jnp.concatenate([total[0:1], total[64:65]] * 4, axis=0)
+    send[...] = ctx[rows(1 - core, HALF)]
+
+
+def call_forward(ids, q, k, v):
+    pair = pl.BlockSpec((1024, 128), lambda p: (0, p))
+    return pl.pallas_call(
+        forward_kernel,
+        grid=(4,),
+        out_shape=(shape(1024, HALF), shape(4, 8, 1024, dtype=f32), shape(HALF, HALF)),
+        in_specs=[SMEM, pair, pair, pair],
+        out_specs=(
+            pair,
+            pl.BlockSpec((1, 8, 1024), lambda p: (p, 0, 0)),
+            pl.BlockSpec((HALF, 128), lambda p: (0, p)),
+        ),
+        compiler_params=params(40),
+        name="attention",
+    )(ids, q, k, v)
+
+
+def backward_kernel(ids, q, k, v, ctx, stat, g_own, g_other, dq, dk, dv, grads, acc_k, acc_v):
+    core = ids[0]
+    grads[rows(core, HALF)] = g_own[...]
+    grads[rows(1 - core, HALF)] = g_other[...]
+    keys = k[...]
+    values = v[...]
+    product = grads[...].astype(f32) * ctx[...].astype(f32)
+    high = product.astype(bf16)
+    rest = (product - high.astype(f32)).astype(bf16)
+    r = lax.broadcasted_iota(jnp.int32, (16, 128), 0)
+    s = lax.broadcasted_iota(jnp.int32, (16, 128), 1)
+    pick = jnp.where((s < 64) == (lax.rem(r, 2) == 0), 1.0, 0.0).astype(bf16)
+    inner = nt(pick, high) + nt(pick, rest)
+    acc_k[...] = jnp.zeros_like(acc_k)
+    acc_v[...] = jnp.zeros_like(acc_v)
+    for i in range(4):
+        ext = (i + 1) * BLOCK
+        cols = slice(i * BLOCK, ext)
+        query = q[cols]
+        grad = grads[cols]
+        mine = low_half(query)
+        zero = jnp.zeros_like(query)
+        new_q = []
+        for a in range(2):
+            if a == 0:
+                part, part_grad = jnp.where(mine, query, zero), jnp.where(mine, grad, zero)
+            else:
+                part, part_grad = jnp.where(mine, zero, query), jnp.where(mine, zero, grad)
+            scores = nt(keys[:ext], part)
+            probs = jnp.exp(scores - stat[0, a : a + 1, cols])
+            last = probs[i * BLOCK :]
+            r = lax.broadcasted_iota(jnp.int32, last.shape, 0)
+            s = lax.broadcasted_iota(jnp.int32, last.shape, 1)
+            last = jnp.where(r <= s, last, 0.0)
+            probs = jnp.concatenate([probs[: i * BLOCK], last], axis=0) if i else last
+            grad_probs = nt(values[:ext], part_grad)
+            grad_scores = (probs * (grad_probs - inner[a : a + 1, cols])).astype(bf16)
+            acc_v[:ext] += nn(probs.astype(bf16), part_grad)
+            acc_k[:ext] += nn(grad_scores, part)
+            new_q.append(tn(grad_scores, keys[:ext]))
+        both = jnp.where(low_half(new_q[0]), new_q[0], new_q[1])
+        dq[cols] = (both * 0.125).astype(bf16)
+    dk[...] = acc_k[...].astype(bf16)
+    dv[...] = acc_v[...].astype(bf16)
+
+
+def call_backward(ids, q, k, v, ctx, stat, g_own, g_other):
+    pair = pl.BlockSpec((1024, 128), lambda p: (0, p))
+    half = pl.BlockSpec((HALF, 128), lambda p: (0, p))
+    return pl.pallas_call(
+        backward_kernel,
+        grid=(4,),
+        out_shape=(shape(1024, HALF),) * 3,
+        in_specs=[SMEM, pair, pair, pair, pair, pl.BlockSpec((1, 8, 1024), lambda p: (p, 0, 0)), half, half],
+        out_specs=(pair,) * 3,
+        scratch_shapes=[
+            pltpu.VMEM((1024, 128), bf16),
+            pltpu.VMEM((1024, 128), f32),
+            pltpu.VMEM((1024, 128), f32),
+        ],
+        compiler_params=params(40),
+        name="attention_back",
+    )(ids, q, k, v, ctx, stat, g_own, g_other)
+
+
+def start_pieces(go, pieces, target, chip, size):
+    own, by_x, by_y, top, low = pieces
+    return [
+        go.start(own, target.at[rows(chip, size)]),
+        go.start(by_x, target.at[rows(chip ^ 1, size)]),
+        go.start(by_y, target.at[rows(chip ^ 2, size)]),
+        go.start(top, target.at[rows(2 * (chip ^ 3), size // 2)]),
+        go.start(low, target.at[rows(2 * (chip ^ 3) + 1, size // 2)]),
+    ]
+
+
+def start_tokens(go, pair, target, z):
+    return [go.start(ref, target.at[rows(parity(z, k), BLOCK)]) for k, ref in enumerate(pair)]
+
+
+def middle_kernel(*refs):
+    ids, ctx, other = refs[:3]
+    mine, theirs = refs[3:8], refs[8:13]
+    x0, x1, bias, gain, shift, middle, normed, w_out, cs, ws, xs, sems = refs[13:]
+    core, z, chip = ids[0], ids[1], ids[2]
+    go = Copies(sems)
+    arrive = [go.start(ctx.at[rows(core, HALF)], cs)]
+    arrive += start_pieces(go, mine, ws.at[0], chip, 128)
+    arrive += start_pieces(go, theirs, ws.at[1], chip, 128)
+    arrive += start_tokens(go, (x0, x1), xs, z)
+    wait_all(arrive)
+    keep = go.start(ws, w_out)
+
+    @pl.loop(0, 2)
+    def _(i):
+        at = rows(i, BLOCK)
+        value = nn(cs[at], ws[0]) + nn(other[at], ws[1])
+        value = value + xs[at].astype(f32) + bias[...]
+        middle[at] = value
+        hat, _ = center_scale(value)
+        normed[at] = (hat * gain[...] + shift[...]).astype(bf16)
+
+    keep.wait()
+
+
+def call_middle(ids, ctx, other, mine, theirs, x_own, bias, gain, shift):
+    return pl.pallas_call(
+        middle_kernel,
+        out_shape=(shape(HALF, 1024, dtype=f32), shape(HALF, 1024), shape(2, HALF, 1024)),
+        in_specs=[SMEM, HBM, VMEM] + [HBM] * 12 + [VMEM] * 3,
+        out_specs=(VMEM, VMEM, HBM),
+        scratch_shapes=[
+            pltpu.VMEM((HALF, HALF), bf16),
+            pltpu.VMEM((2, HALF, 1024), bf16),
+            pltpu.VMEM((HALF, 1024), bf16),
+            pltpu.SemaphoreType.DMA((14,)),
+        ],
+        compiler_params=params(32),
+        name="middle",
+    )(ids, ctx, other, *mine, *theirs, *x_own, bias, gain, shift)
+
+
+def hidden_kernel(*refs):
+    ids, normed = refs[:2]
+    mine, theirs = refs[2:7], refs[7:12]
+    bias, active, slope, w_out, ws, sems = refs[12:]
+    core, chip = ids[0], ids[2]
+    go = Copies(sems)
+    arrive = []
+    for side, pieces in ((core, mine), (1 - core, theirs)):
+        own, by_x, by_y, top, low = pieces
+        for r, ref in enumerate((own, by_x, by_y)):
+            arrive.append(go.start(ref, ws.at[rows(2 * (chip ^ r) + side, 128)]))
+        arrive.append(go.start(top, ws.at[rows(4 * (chip ^ 3) + 2 * side, 64)]))
+        arrive.append(go.start(low, ws.at[rows(4 * (chip ^ 3) + 2 * side + 1, 64)]))
+    wait_all(arrive)
+    keep = [go.start(ws.at[:, d * HALF : (d + 1) * HALF], w_out.at[d]) for d in range(8)]
+    for d in range(8):
+        cols = slice(d * HALF, (d + 1) * HALF)
+
+        @pl.loop(0, 2)
+        def _(i):
+            at = rows(i, BLOCK)
+            h = nn(normed[at], ws[:, cols]) + bias[:, cols]
+            square = h * h
+            t = jnp.tanh(h * (GELU_A + (GELU_A * GELU_B) * square))
+            lift = 0.5 + 0.5 * t
+            active[d, at] = (h * lift).astype(bf16)
+            inner = GELU_A + (3.0 * GELU_A * GELU_B) * square
+            slope[d, at] = (lift + (0.5 * h) * (1.0 - t * t) * inner).astype(bf16)
+
+    wait_all(keep)
+
+
+def call_hidden(ids, normed, mine, theirs, bias):
+    return pl.pallas_call(
+        hidden_kernel,
+        out_shape=(shape(8, HALF, HALF), shape(8, HALF, HALF), shape(8, 1024, HALF)),
+        in_specs=[SMEM, VMEM] + [HBM] * 10 + [VMEM],
+        out_specs=(VMEM, VMEM, HBM),
+        scratch_shapes=[pltpu.VMEM((1024, 4096), bf16), pltpu.SemaphoreType.DMA((18,))],
+        compiler_params=params(48),
+        name="hidden",
+    )(ids, normed, *mine, *theirs, bias)
+
+
+def feed_kernel(steps, first, *refs):
+    n = len(steps)
+    ids, g0, g1, active, slope, w_in = refs[:6]
+    pieces = refs[6 : 6 + n]
+    refs = refs[6 + n :]
+    if not first:
+        old_result, old_grad, refs = refs[0], refs[1], refs[2:]
+    result, grad, gs, acts, slopes, w_ins, w_outs, sems = refs[:8]
+    core, z, chip = ids[0], ids[1], ids[2]
+    go = Copies(sems)
+    tokens = start_tokens(go, (g0, g1), gs, z)
+    copies = []
+    for at, (r, side) in enumerate(steps):
+        d = 2 * (chip ^ r) + (core ^ side)
+        copies.append(
+            [
+                go.start(pieces[at], w_outs.at[at]),
+                go.start(slope.at[d], slopes.at[at]),
+                go.start(w_in.at[d], w_ins.at[at]),
+                go.start(active.at[d], acts.at[at]),
+            ]
+        )
+    wait_all(tokens)
+    for at in range(n):
+        wait_all(copies[at])
+
+        @pl.loop(0, 2)
+        def _(i):
+            tok = rows(i, BLOCK)
+            back = nt(gs[tok], w_outs[at]) * slopes[at, tok].astype(f32)
+            more = nt(back.astype(bf16), w_ins[at])
+            out = nn(acts[at, tok], w_outs[at])
+            if at == 0:
+                if first:
+                    grad[tok] = more
+                    result[tok] = out
+                else:
+                    grad[tok] = old_grad[tok] + more
+                    result[tok] = old_result[tok] + out
+            else:
+                grad[tok] += more
+                result[tok] += out
+
+
+def call_feed(ids, steps, g_own, active, slope, w_in, pieces, old):
+    n = len(steps)
+    first = old is None
+    return pl.pallas_call(
+        functools.partial(feed_kernel, steps, first),
+        out_shape=(shape(HALF, 1024, dtype=f32),) * 2,
+        in_specs=[SMEM] + [HBM] * (5 + n) + ([] if first else [VMEM, VMEM]),
+        out_specs=(VMEM, VMEM),
+        scratch_shapes=[
+            pltpu.VMEM((HALF, 1024), bf16),
+            pltpu.VMEM((n, HALF, HALF), bf16),
+            pltpu.VMEM((n, HALF, HALF), bf16),
+            pltpu.VMEM((n, 1024, HALF), bf16),
+            pltpu.VMEM((n, HALF, 1024), bf16),
+            pltpu.SemaphoreType.DMA((2 + 4 * n,)),
+        ],
+        compiler_params=params(48),
+        name="feed",
+    )(ids, *g_own, active, slope, w_in, *pieces, *(() if first else old))
+
+
+def last_grad_kernel(
+    ids, g0, g1, slope, w_in, wt0, wl0, wt1, wl1, old_grad, middle, gain, w_o,
+    grad_middle, ctx_own, ctx_send, gs, slopes, w_ins, w_outs, sems,
+):
+    core, z, chip = ids[0], ids[1], ids[2]
+    go = Copies(sems)
+    tokens = start_tokens(go, (g0, g1), gs, z)
+    copies = []
+    for at, (top, low) in enumerate(((wt0, wl0), (wt1, wl1))):
+        d = 2 * (chip ^ 3) + (core ^ at)
+        copies.append(
+            [
+                go.start(top, w_outs.at[at, :BLOCK]),
+                go.start(low, w_outs.at[at, BLOCK:]),
+                go.start(slope.at[d], slopes.at[at]),
+                go.start(w_in.at[d], w_ins.at[at]),
+            ]
+        )
+    wait_all(tokens)
+    wait_all(copies[0])
+    wait_all(copies[1])
+
+    @pl.loop(0, 2)
+    def _(i):
+        tok = rows(i, BLOCK)
+        grad = old_grad[tok]
+        for at in range(2):
+            back = nt(gs[tok], w_outs[at]) * slopes[at, tok].astype(f32)
+            grad += nt(back.astype(bf16), w_ins[at])
+        hat, inverse = center_scale(middle[tok])
+        value = gs[tok].astype(f32) + norm_back(hat, inverse, grad * gain[...])
+        grad_middle[tok] = value
+        low_value = value.astype(bf16)
+        ctx_own[tok] = nt(low_value, w_o[0]).astype(bf16)
+        ctx_send[tok] = nt(low_value, w_o[1]).astype(bf16)
+
+
+def call_last_grad(ids, g_own, slope, w_in, halves, old_grad, middle, gain, w_o):
+    return pl.pallas_call(
+        last_grad_kernel,
+        out_shape=(shape(HALF, 1024, dtype=f32), shape(HALF, HALF), shape(HALF, HALF)),
+        in_specs=[SMEM] + [HBM] * 8 + [VMEM] * 4,
+        out_specs=(VMEM,) * 3,
+        scratch_shapes=[
+            pltpu.VMEM((HALF, 1024), bf16),
+            pltpu.VMEM((2, HALF, HALF), bf16),
+            pltpu.VMEM((2, 1024, HALF), bf16),
+            pltpu.VMEM((2, HALF, 1024), bf16),
+            pltpu.SemaphoreType.DMA((10,)),
+        ],
+        compiler_params=params(48),
+        name="middle_grad",
+    )(ids, *g_own, slope, w_in, *halves, old_grad, middle, gain, w_o)
+
+
+def last_result_kernel(
+    ids, active, wt0, wl0, wt1, wl1, old_result, middle, bias, out0, out1, acts, w_outs, sems
+):
+    core, z, chip = ids[0], ids[1], ids[2]
+    go = Copies(sems)
+    arrive = []
+    for at, (top, low) in enumerate(((wt0, wl0), (wt1, wl1))):
+        d = 2 * (chip ^ 3) + (core ^ at)
+        arrive.append(go.start(top, w_outs.at[at, :BLOCK]))
+        arrive.append(go.start(low, w_outs.at[at, BLOCK:]))
+        arrive.append(go.start(active.at[d], acts.at[at]))
+    wait_all(arrive)
+    for k, out in enumerate((out0, out1)):
+        tok = rows(parity(z, k), BLOCK)
+        value = old_result[tok] + middle[tok] + bias[...]
+        for at in range(2):
+            value += nn(acts[at, tok], w_outs[at])
+        out[...] = value.astype(bf16)
+
+
+def call_last_result(ids, active, halves, old_result, middle, bias):
+    return pl.pallas_call(
+        last_result_kernel,
+        out_shape=(shape(BLOCK, 1024),) * 2,
+        in_specs=[SMEM] + [HBM] * 5 + [VMEM] * 3,
+        out_specs=(VMEM,) * 2,
+        scratch_shapes=[
+            pltpu.VMEM((2, HALF, HALF), bf16),
+            pltpu.VMEM((2, HALF, 1024), bf16),
+            pltpu.SemaphoreType.DMA((6,)),
+        ],
+        compiler_params=params(32),
+        name="result",
+    )(ids, active, *halves, old_result, middle, bias)
+
+
+def qkv_back_kernel(
+    ids, dq, dk, dv, w, normed, down, down_w, up_w, own, send, g_norm, g_up, tilt_acc, up_acc
+):
+    core = ids[0]
+    tilt_acc[...] = jnp.zeros_like(tilt_acc)
+    up_acc[...] = jnp.zeros_like(up_acc)
+
+    @pl.loop(0, 4)
+    def _(i):
+        at = rows(i, BLOCK)
+        gq, gk, gv = dq[at], dk[at], dv[at]
+        tilt = (nt(gq, up_w[:, :HALF]) + nt(gv, up_w[:, 2 * HALF :])).astype(bf16)
+        value = nt(gq, w[:, :HALF]) + nt(gk, w[:, HALF : 2 * HALF]) + nt(gv, w[:, 2 * HALF :])
+        value = (value + nn(tilt, down_w[...])).astype(bf16)
+        place = rows(lax.rem(i, 2), BLOCK)
+
+        @pl.when(i // 2 == core)
+        def _():
+            own[place] = value
+
+        @pl.when(i // 2 != core)
+        def _():
+            send[place] = value
+
+        tilt_acc[...] += tn(tilt, normed[at])
+        up_acc[:, :HALF] += tn(down[at], gq)
+        up_acc[:, HALF:] += tn(down[at], gv)
+
+    g_norm[...] = tilt_acc[:8]
+    g_up[...] = up_acc[:8]
+
+
+def call_qkv_back(ids, dq, dk, dv, w, normed, down, down_w, up_w):
+    return pl.pallas_call(
+        qkv_back_kernel,
+        out_shape=(
+            shape(HALF, 1024),
+            shape(HALF, 1024),
+            shape(8, 1024, dtype=f32),
+            shape(8, 1024, dtype=f32),
+        ),
+        in_specs=[SMEM] + [VMEM] * 8,
+        out_specs=(VMEM,) * 4,
+        scratch_shapes=[pltpu.VMEM((128, 1024), f32), pltpu.VMEM((128, 1024), f32)],
+        compiler_params=params(40),
+        name="qkv_back",
+    )(ids, dq, dk, dv, w, normed, down, down_w, up_w)
+
+
+def input_grad_kernel(ids, x0, x1, own, other, grad_middle, gain, out0, out1):
+    z = ids[1]
+    for k, (x, out) in enumerate(((x0, out0), (x1, out1))):
+        tok = rows(parity(z, k), BLOCK)
+        grad = own[tok].astype(f32) + other[tok].astype(f32)
+        hat, inverse = center_scale(x[...].astype(f32))
+        out[...] = (grad_middle[tok] + norm_back(hat, inverse, grad * gain[...])).astype(bf16)
+
+
+def call_input_grad(ids, x_own, own, other, grad_middle, gain):
+    return pl.pallas_call(
+        input_grad_kernel,
+        out_shape=(shape(BLOCK, 1024),) * 2,
+        in_specs=[SMEM] + [VMEM] * 6,
+        out_specs=(VMEM,) * 2,
+        compiler_params=params(32),
+        name="input_grad",
+    )(ids, *x_own, own, other, grad_middle, gain)
+
+
+def to_core(value):
+    return lax.ppermute(value, "core", SWAP)
+
+
+def exchange(z, pair):
+    sent = []
+    for k in range(2):
+        perm = [
+            (4 * core + at, 4 * (at // 2) + 2 * core + (at + k) % 2)
+            for core in range(2)
+            for at in range(4)
+        ]
+        sent.append(lax.ppermute(pair[k], ("core", "seq"), perm))
+    return sent
+
+
+def by_parity(z, pair):
+    even = lax.rem(z, 2) == 0
+    return jnp.where(even, pair[0], pair[1]), jnp.where(even, pair[1], pair[0])
+
+
+def gather(shard):
+    by_x = lax.ppermute(shard, "x", SWAP)
+    by_y = lax.ppermute(shard, "y", SWAP)
+    half = shard.shape[0] // 2
+    top = lax.ppermute(by_x[:half], "y", SWAP)
+    low = lax.ppermute(by_y[half:], "x", SWAP)
+    return [shard, by_x, by_y, top, low]
+
+
+def on_chip(
+    inputs,
+    out_grad,
+    norm_gain,
+    norm_bias,
+    proj_bias,
+    fc_bias,
+    qkv_weight,
+    out_weight,
+    feed_input_weight,
+    proj_weight,
+    adapters,
+    first_moment,
+    second_moment,
+):
+    core = lax.axis_index("core")
+    z = lax.axis_index("seq")
+    chip = 2 * lax.axis_index("y") + lax.axis_index("x")
+    ids = jnp.stack([core, z, chip]).astype(jnp.int32)
+
+    by_core = qkv_weight.reshape(128, 12, 2, 128)
+    first, second = by_core[:, :, 0].reshape(128, 1536), by_core[:, :, 1].reshape(128, 1536)
+    kept = jnp.where(core == 0, first, second)
+    passed = jnp.where(core == 0, second, first)
+    got = to_core(passed)
+    qkv_shard = jnp.concatenate(
+        [jnp.where(core == 0, kept, got), jnp.where(core == 0, got, kept)], axis=0
+    )
+    x_own = exchange(z, by_parity(z, (inputs[0], inputs[1])))
+    x_other = [to_core(part) for part in x_own]
+    qkv_pieces = gather(qkv_shard)
+    out_pieces = gather(out_weight)
+    out_other = [to_core(part) for part in out_pieces]
+    in_pieces = gather(feed_input_weight)
+    in_other = [to_core(part) for part in in_pieces]
+    proj_pieces = gather(proj_weight)
+    proj_other = [to_core(part) for part in proj_pieces]
+    g_own = exchange(z, by_parity(z, (out_grad[0], out_grad[1])))
+
+    def columns(value):
+        lead = value.shape[0]
+        value = value.reshape(lead, 4, 2, 128)
+        return jnp.where(core == 0, value[:, :, 0], value[:, :, 1]).reshape(lead, HALF)
+
+    scale = adapter_alpha / ADAPTER_RANK
+    up_q, up_v = scale * columns(adapters[1]), scale * columns(adapters[3])
+    up_w = jnp.zeros((128, 1536), f32)
+    up_w = up_w.at[0:4, :HALF].set(up_q).at[4:8, 2 * HALF :].set(up_v).astype(bf16)
+    down_w = jnp.concatenate([adapters[0], adapters[2], jnp.zeros((120, 1024), f32)], axis=0)
+    down_w = down_w.astype(bf16)
+    head_bias = columns(proj_bias[:2])
+    qkv_bias = jnp.concatenate([head_bias[0], jnp.zeros((HALF,), f32), head_bias[1]])[None]
+
+    q, k, v, normed, down, qkv_full = call_qkv(
+        ids, x_own, x_other, qkv_pieces, norm_gain[:1], norm_bias[:1], down_w, up_w, qkv_bias
+    )
+    ctx, stat, ctx_send = call_forward(ids, q, k, v)
+    ctx_other = to_core(ctx_send)
+    middle, normed_two, out_full = call_middle(
+        ids, ctx, ctx_other, out_pieces, out_other, x_own, proj_bias[2:3], norm_gain[1:], norm_bias[1:]
+    )
+    active, slope, w_in = call_hidden(ids, normed_two, in_pieces, in_other, fc_bias[None])
+    old = call_feed(
+        ids, ((0, 0), (0, 1)), g_own, active, slope, w_in, (proj_pieces[0], proj_other[0]), None
+    )
+    result, grad = call_feed(
+        ids,
+        ((1, 0), (1, 1), (2, 0), (2, 1)),
+        g_own,
+        active,
+        slope,
+        w_in,
+        (proj_pieces[1], proj_other[1], proj_pieces[2], proj_other[2]),
+        old,
+    )
+    halves = (proj_pieces[3], proj_pieces[4], proj_other[3], proj_other[4])
+    grad_middle, grad_ctx, grad_send = call_last_grad(
+        ids, g_own, slope, w_in, halves, grad, middle, norm_gain[1:], out_full
+    )
+    grad_ctx_other = to_core(grad_send)
+    mixed = exchange(z, call_last_result(ids, active, halves, result, middle, proj_bias[3:]))
+    dq, dk, dv = call_backward(ids, q, k, v, ctx, stat, grad_ctx, grad_ctx_other)
+    own, send, g_norm, g_up = call_qkv_back(
+        ids, dq, dk, dv, qkv_full, normed, down, down_w, up_w
+    )
+    other = to_core(send)
+    grad_in = exchange(z, call_input_grad(ids, x_own, own, other, grad_middle, norm_gain[:1]))
+
+    def spread(part):
+        part = part.reshape(4, 4, 1, 128)
+        place = lax.broadcasted_iota(jnp.int32, (1, 1, 2, 1), 2)
+        return jnp.where(place == core, part, 0.0).reshape(4, 1024)
+
+    total = jnp.stack(
+        [
+            g_norm[:4],
+            scale * spread(g_up[:4, :HALF]),
+            g_norm[4:],
+            scale * spread(g_up[4:, HALF:]),
+        ]
+    )
+    for axis, perm in (
+        ("core", SWAP),
+        ("x", SWAP),
+        ("y", SWAP),
+        ("seq", ((0, 1), (1, 0), (2, 3), (3, 2))),
+        ("seq", ((0, 2), (2, 0), (1, 3), (3, 1))),
+    ):
+        total = total + lax.ppermute(total, axis, perm)
+    grad_norm = jnp.sqrt(jnp.sum(total * total))
+    clipped, new_weight, new_first, new_second = adam_update(
+        total, adapters, first_moment, second_moment, grad_norm
+    )
+    mixed = jnp.stack(by_parity(z, mixed))
+    grad_input = jnp.stack(by_parity(z, grad_in))
+    return (mixed, grad_input, clipped, grad_norm, new_weight, new_first, new_second)
+
+
 def solution(mesh):
+    sizes = dict(mesh.shape)
+    if sizes["dp"] == 8 and sizes["seq"] == 4:
+        plane = Mesh(mesh.devices.reshape(2, 2, 2, 4), ("y", "x", "core", "seq"))
+        return build(plane, ("y", "x", "core"), on_chip)
+    return build(mesh, "dp", on_device)
+
+
+def build(mesh, dp, step):
+    tokens, weight = P(dp, "seq", None), P(dp, None)
     return jax.shard_map(
-        on_device,
+        step,
         mesh=mesh,
-        in_specs=(
-            P("dp", "seq", None),
-            P("dp", "seq", None),
-            P(),
-            P(),
-            P(),
-            P(),
-            P("dp", None),
-            P("dp", None),
-            P("dp", None),
-            P("dp", None),
-            P(),
-            P(),
-            P(),
-        ),
-        out_specs=(P("dp", "seq", None), P("dp", "seq", None), P(), P(), P(), P(), P()),
+        in_specs=(tokens, tokens) + (P(),) * 4 + (weight,) * 4 + (P(),) * 3,
+        out_specs=(tokens, tokens) + (P(),) * 5,
         check_vma=False,
     )

time: 884 us -> 353 us (0.40); the launches traced: 874 us -> 352 us
  waiting for transfers between devices: 397 us -> 134 us
  matrix products: 184 us -> 0 us
  local copies, waits for them, and re-layouts: 161 us -> 43.5 us
  Pallas kernels: 0 us -> 111 us
  other arithmetic: 78.2 us -> 10.6 us
  between operations: 16.6 us -> 3.53 us
  starting transfers between devices: 36.7 us -> 49.2 us
    dot_general x57 -> x0, matrix products: 184 us -> none  [the longest x4 40.8 us: dot_trans(): lax.dot_general(left, right, (((1,), (1,)), ((), ())), preferred_element_...]
    all_gather x4 -> x0, waiting for transfers between devices: 171 us -> none  [the longest x1 56.3 us: on_device(): lax.all_gather(feed_input_weight, 'dp', axis=0, tiled=True)]
    ppermute x0 -> x50, waiting for transfers between devices: none -> 134 us  [the longest x8 53.1 us: exchange(): sent.append(lax.ppermute(pair[k], ('core', 'seq'), perm))]
    psum x1 -> x0, waiting for transfers between devices: 118 us -> none  [on_device(): total = lax.psum(partial_terms, ('dp', 'seq'))]
    pallas_call x0 -> x11, Pallas kernels: none -> 111 us  [the longest x2 23.1 us: call_feed(): pl.pallas_call(functools.partial(feed_kernel, steps, first), out_shape=(s...]
    all_to_all x6 -> x0, waiting for transfers between devices: 106 us -> none  [the longest x2 56.5 us: forward(): lax.all_to_all(joined, 'seq', split_axis=3, concat_axis=1, tiled=True)]
    while x108 -> x0, local copies, waits for them, and re-layouts: 60.2 us -> none
    ppermute x0 -> x50, starting transfers between devices: none -> 49.2 us  [the longest x8 20.5 us: exchange(): sent.append(lax.ppermute(pair[k], ('core', 'seq'), perm))]
  transfers between devices with their start and end apart: 11 -> 50, of which waited for: 8 -> 21; matrix products, arithmetic and copies ran while one was open for 34% -> 6% of each run, Pallas kernels for 0% -> 21%
where the time goes in v1:
time: 353 us; the launch traced here: 352 us
  waiting for transfers between devices  134 us (38%)
  Pallas kernels  111 us (31%)
  starting transfers between devices  49.2 us (14%)
  local copies, waits for them, and re-layouts  43.5 us (12%)
  other arithmetic  10.6 us (3%)
    ppermute x8, waiting for transfers between devices, exchange(): sent.append(lax.ppermute(pair[k], ('core', 'seq'), perm))  53.1 us
    unnamed x150, local copies, waits for them, and re-layouts  31.3 us
    pallas_call x2, Pallas kernels, call_feed(): pl.pallas_call(functools.partial(feed_kernel, steps, first), out_shape=(s...  23.1 us
    ppermute x4, waiting for transfers between devices, gather(): low = lax.ppermute(by_y[half:], 'x', SWAP)  22.5 us
    ppermute x4, waiting for transfers between devices, gather(): by_y = lax.ppermute(shard, 'y', SWAP)  22.3 us
    ppermute x8, starting transfers between devices, exchange(): sent.append(lax.ppermute(pair[k], ('core', 'seq'), perm))  20.5 us
    pallas_call x1, Pallas kernels, call_backward(): pl.pallas_call(backward_kernel, grid=(4,), out_shape=(shape(1024, HALF),)...  18.2 us
    pallas_call x1, Pallas kernels, call_hidden(): pl.pallas_call(hidden_kernel, out_shape=(shape(8, HALF, HALF), shape(8, H...  17.9 us
  transfers between devices with their start and end apart: 50, of which 21 were waited for; matrix products, arithmetic and copies ran while one was open for 6% of the time, Pallas kernels for 21%

profile of v1, /device:TPU:9, one launch (start us, length us, event | category | flops | bytes accessed | tf_op | source)
XLA Modules:
  0.0 351.9 jit_solution(1106423470794151544)
XLA Ops:
  8.7 4.6 %collective-permute-start = (bf16[256,1024]{1,0:T(8,128)(2,1)}, bf16[256,1024]{1,0:T(8,128)(2,1)S(1)}, u32[]{:S(2)}, u32[]{:S(2)}) collective-permute-start(bf16[256,1024]{1,0:T(8,128)(2,1)} %get-tuple-element.110), channel_id=1, source_target_pairs={{0,0},{1,1},{2,4},{3,5},{4,2},{5,3},{6,6},{7,7},{8,8},{9,9},{10,12... | collective-permute-start | bytes 1572872 | tf_op jit(solution)/shard_map/ppermute | solution.py:891
  13.3 2.3 select_bitcast_fusion.4
  16.4 3.6 %collective-permute-done.12.refs_6_ = bf16[64,1024]{1,0:T(8,128)(2,1)S(1)} collective-permute-done((bf16[64,1024]{1,0:T(8,128)(2,1)S(1)}, bf16[64,1024]{1,0:T(8,128)(2,1)S(1)}, u32[]{:S(2)}, u32[]{:S(2)}) %collective-permute-start.12) | collective-permute-done | bytes 131104 | tf_op jit(solution)/shard_map/ppermute | solution.py:904
  20.4 22.5 %collective-permute-done.13.refs_7_ = bf16[64,1024]{1,0:T(8,128)(2,1)S(1)} collective-permute-done((bf16[64,1024]{1,0:T(8,128)(2,1)S(1)}, bf16[64,1024]{1,0:T(8,128)(2,1)S(1)}, u32[]{:S(2)}, u32[]{:S(2)}) %collective-permute-start.13) | collective-permute-done | bytes 131104 | tf_op jit(solution)/shard_map/ppermute | solution.py:905
  42.9 3.3 collective-permute-start.34
  53.7 5.6 %collective-permute-done.34.refs_1_.g0 = bf16[256,1024]{1,0:T(8,128)(2,1)S(1)} collective-permute-done((bf16[256,1024]{1,0:T(8,128)(2,1)}, bf16[256,1024]{1,0:T(8,128)(2,1)S(1)}, u32[]{:S(2)}, u32[]{:S(2)}) %collective-permute-start.34) | collective-permute-done | bytes 524320 | tf_op jit(solution)/shard_map/ppermute | solution.py:891
  60.7 11.1 %collective-permute-done.35.refs_2_.g1 = bf16[256,1024]{1,0:T(8,128)(2,1)S(1)} collective-permute-done((bf16[256,1024]{1,0:T(8,128)(2,1)}, bf16[256,1024]{1,0:T(8,128)(2,1)S(1)}, u32[]{:S(2)}, u32[]{:S(2)}) %collective-permute-start.35) | collective-permute-done | bytes 524320 | tf_op jit(solution)/shard_map/ppermute | solution.py:891
  73.3 3.0 collective-permute-done.20.refs_4_
  78.1 16.8 %collective-permute-done.5.w1 = bf16[256,1536]{1,0:T(8,128)(2,1)} collective-permute-done((bf16[256,1536]{1,0:T(8,128)(2,1)S(1)}, bf16[256,1536]{1,0:T(8,128)(2,1)}, u32[]{:S(2)}, u32[]{:S(2)}) %collective-permute-start.5) | collective-permute-done | bytes 786464 | tf_op jit(solution)/shard_map/ppermute | solution.py:901
  96.2 19.4 %collective-permute-done.6.w2 = bf16[256,1536]{1,0:T(8,128)(2,1)} collective-permute-done((bf16[256,1536]{1,0:T(8,128)(2,1)S(1)}, bf16[256,1536]{1,0:T(8,128)(2,1)}, u32[]{:S(2)}, u32[]{:S(2)}) %collective-permute-start.6) | collective-permute-done | bytes 786464 | tf_op jit(solution)/shard_map/ppermute | solution.py:902
  129.7 2.6 collective-permute-done.7.w3t
  135.2 8.8 %qkv.1 = (bf16[1024,512]{1,0:T(8,128)(2,1)S(1)}, bf16[1024,512]{1,0:T(8,128)(2,1)S(1)}, bf16[1024,512]{1,0:T(8,128)(2,1)S(1)}, bf16[1024,1024]{1,0:T(8,128)(2,1)...) custom-call(s32[3]{0:T(128)S(1)} %pad_add_fusion.ids.refs_0_, ...), custom_call_target="tpu_custom_call" | custom-call | tf_op jit(solution)/shard_map/qkv/pallas_call | solution.py:410
  146.2 14.5 %attention.1 = (bf16[1024,512]{1,0:T(8,128)(2,1)S(1)}, f32[4,8,1024]{2,1,0:T(8,128)S(1)}, bf16[512,512]{1,0:T(8,128)(2,1)S(1)}) custom-call(s32[3]{0:T(128)S(1)} %pad_add_fusion.ids.refs_0_, bf16[1024,512]{1,0:T(8,128)(2,1)S(1)} %get-tuple-element.64.q, bf16[1024,512]{1,0:T(8,128)(2,1)S(1)} %get-tuple-element.65.k, bf16[1024,512]{1,0:T(8,128)(2,1)S(1)} %get-tuple-element.66.v), custom_call_target="tpu_custom_call" | custom-call | tf_op jit(solution)/shard_map/attention/pallas_call | solution.py:473
  169.9 3.8 %middle.1 = (f32[512,1024]{1,0:T(8,128)S(1)}, bf16[512,1024]{1,0:T(8,128)(2,1)S(1)}, bf16[2,512,1024]{2,1,0:T(8,128)(2,1)S(1)}) custom-call(s32[3]{0:T(128)S(1)} %pad_add_fusion.ids.refs_0_, bf16[1024,512]{1,0:T(8,128)(2,1)S(1)} %get-tuple-element.67.refs_1_.ctx, bf16[512,512]{1,0:T(8,128)(2,1)S(1)} %collective-permute-done.9.refs_2_, ...), custom_call_target="tpu_custom_call" | custom-call | tf_op jit(solution)/shard_map/middle/pallas_call | solution.py:594
  177.5 17.9 %hidden.1 = (bf16[8,512,512]{2,1,0:T(8,128)(2,1)}, bf16[8,512,512]{2,1,0:T(8,128)(2,1)}, bf16[8,1024,512]{2,1,0:T(8,128)(2,1)}) custom-call(s32[3]{0:T(128)S(1)} %pad_add_fusion.ids.refs_0_, bf16[512,1024]{1,0:T(8,128)(2,1)S(1)} %get-tuple-element.69.refs_1_, bf16[128,4096]{1,0:T(8,128)(2,1)} %refs_2_.1, bf16[128,4096]{1,0:T(8,128)(2,1)} %collective-permute-done.19.refs_3_, ...), custom_call_target="tpu_custom_call" | custom-call | tf_op jit(solution)/shard_map/hidden/pallas_call | solution.py:643
  195.4 8.3 %feed.2 = (f32[512,1024]{1,0:T(8,128)S(1)}, f32[512,1024]{1,0:T(8,128)}) custom-call(s32[3]{0:T(128)S(1)} %pad_add_fusion.ids.refs_0_, bf16[256,1024]{1,0:T(8,128)(2,1)S(1)} %collective-permute-done.34.refs_1_.g0, bf16[256,1024]{1,0:T(8,128)(2,1)S(1)} %collective-permute-done.35.refs_2_.g1, bf16[8,512,512]{2,1,0:T(8,128)(2,1)} %get-tuple-element.70.refs_3_.active, ...), custom_call_target="tpu_custom_call" | custom-call | tf_op jit(solution)/shard_map/feed/pallas_call | solution.py:701
  205.1 14.8 %feed.3 = (f32[512,1024]{1,0:T(8,128)}, f32[512,1024]{1,0:T(8,128)}) custom-call(s32[3]{0:T(128)S(1)} %pad_add_fusion.ids.refs_0_, bf16[256,1024]{1,0:T(8,128)(2,1)S(1)} %collective-permute-done.34.refs_1_.g0, bf16[256,1024]{1,0:T(8,128)(2,1)S(1)} %collective-permute-done.35.refs_2_.g1, bf16[8,512,512]{2,1,0:T(8,128)(2,1)} %get-tuple-element.70.refs_3_.active, ...), custom_call_target="tpu_custom_call" | custom-call | tf_op jit(solution)/shard_map/feed/pallas_call | solution.py:701
  219.9 11.2 %middle_grad.1 = (f32[512,1024]{1,0:T(8,128)}, bf16[512,512]{1,0:T(8,128)(2,1)S(1)}, bf16[512,512]{1,0:T(8,128)(2,1)}) custom-call(s32[3]{0:T(128)S(1)} %pad_add_fusion.ids.refs_0_, bf16[256,1024]{1,0:T(8,128)(2,1)S(1)} %collective-permute-done.34.refs_1_.g0, bf16[256,1024]{1,0:T(8,128)(2,1)S(1)} %collective-permute-done.35.refs_2_.g1, ...), custom_call_target="tpu_custom_call" | custom-call | tf_op jit(solution)/shard_map/middle_grad/pallas_call | solution.py:757
  239.8 18.2 %attention_back.1 = (bf16[1024,512]{1,0:T(8,128)(2,1)S(1)}, bf16[1024,512]{1,0:T(8,128)(2,1)S(1)}, bf16[1024,512]{1,0:T(8,128)(2,1)S(1)}) custom-call(s32[3]{0:T(128)S(1)} %pad_add_fusion.ids.refs_0_, bf16[1024,512]{1,0:T(8,128)(2,1)S(1)} %get-tuple-element.64.q, bf16[1024,512]{1,0:T(8,128)(2,1)S(1)} %copy-done.4, bf16[1024,512]{1,0:T(8,128)(2,1)S(1)} %copy-done.6, ...), custom_call_target="tpu_custom_call" | custom-call | tf_op jit(solution)/shard_map/attention_back/pallas_call | solution.py:537
  259.6 8.4 %qkv_back.1 = (bf16[512,1024]{1,0:T(8,128)(2,1)S(1)}, bf16[512,1024]{1,0:T(8,128)(2,1)S(1)}, f32[8,1024]{1,0:T(8,128)S(1)}, f32[8,1024]{1,0:T(8,128)S(1)}) custom-call(s32[3]{0:T(128)S(1)} %pad_add_fusion.ids.refs_0_, bf16[1024,512]{1,0:T(8,128)(2,1)S(1)} %get-tuple-element.84.dq, bf16[1024,512]{1,0:T(8,128)(2,1)S(1)} %get-tuple-element.85.dk, ...), custom_call_target="tpu_custom_call" | custom-call | tf_op jit(solution)/shard_map/qkv_back/pallas_call | solution.py:843
  274.8 2.3 collective-permute-done.46
  277.4 2.9 collective-permute-done.47
  281.5 2.0 collective-permute-done.48
  285.6 2.2 copy-done
  293.5 3.0 result.1
  296.5 5.8 %collective-permute-start.39 = (bf16[256,1024]{1,0:T(8,128)(2,1)}, bf16[256,1024]{1,0:T(8,128)(2,1)S(1)}, u32[]{:S(2)}, u32[]{:S(2)}) collective-permute-start(bf16[256,1024]{1,0:T(8,128)(2,1)} %get-tuple-element.77), channel_id=1, source_target_pairs={{0,0},{1,1},{2,4},{3,5},{4,2},{5,3},{6,6},{7,7},{8,8},{9,9},{10,12... | collective-permute-start | bytes 1572872 | tf_op jit(solution)/shard_map/ppermute | solution.py:891
  302.4 2.2 input_grad.1
  304.6 5.3 %collective-permute-start.43 = (bf16[256,1024]{1,0:T(8,128)(2,1)S(1)}, bf16[256,1024]{1,0:T(8,128)(2,1)S(1)}, u32[]{:S(2)}, u32[]{:S(2)}) collective-permute-start(bf16[256,1024]{1,0:T(8,128)(2,1)S(1)} %get-tuple-element.93), channel_id=1, source_target_pairs={{0,0},{1,1},{2,4},{3,5},{4,2},{5,3},{6,6},{7,7},{8,8},{9,9},{10,12... | collective-permute-start | bytes 1572872 | tf_op jit(solution)/shard_map/ppermute | solution.py:891
  312.2 2.8 collective-permute-done.39
  315.0 22.3 %collective-permute-done.40 = bf16[256,1024]{1,0:T(8,128)(2,1)S(1)} collective-permute-done((bf16[256,1024]{1,0:T(8,128)(2,1)}, bf16[256,1024]{1,0:T(8,128)(2,1)S(1)}, u32[]{:S(2)}, u32[]{:S(2)}) %collective-permute-start.40) | collective-permute-done | bytes 524320 | tf_op jit(solution)/shard_map/ppermute | solution.py:891
  337.3 5.0 %collective-permute-done.43 = bf16[256,1024]{1,0:T(8,128)(2,1)S(1)} collective-permute-done((bf16[256,1024]{1,0:T(8,128)(2,1)S(1)}, bf16[256,1024]{1,0:T(8,128)(2,1)S(1)}, u32[]{:S(2)}, u32[]{:S(2)}) %collective-permute-start.43) | collective-permute-done | bytes 524320 | tf_op jit(solution)/shard_map/ppermute | solution.py:891
  342.3 6.3 %collective-permute-done.44 = bf16[256,1024]{1,0:T(8,128)(2,1)S(1)} collective-permute-done((bf16[256,1024]{1,0:T(8,128)(2,1)S(1)}, bf16[256,1024]{1,0:T(8,128)(2,1)S(1)}, u32[]{:S(2)}, u32[]{:S(2)}) %collective-permute-start.44) | collective-permute-done | bytes 524320 | tf_op jit(solution)/shard_map/ppermute | solution.py:891
  (292 shorter events, 85.7 us)
Async XLA Ops:
  0.6 15.0 %collective-permute-start.10 = (bf16[128,1024]{1,0:T(8,128)(2,1)}, bf16[128,1024]{1,0:T(8,128)(2,1)S(1)}, u32[]{:S(2)}, u32[]{:S(2)}) collective-permute-start(bf16[128,1024]{1,0:T(8,128)(2,1)} %refs_3_.1), channel_id=1, source_target_pairs={{0,8},{8,0},{1,9},{9,1},{2,10},{10,2},{3,11},{11,3},{4,12},{12,4},... | collective-permute-start | bytes 786440 | tf_op jit(solution)/shard_map/ppermute | solution.py:901
  1.9 13.8 %collective-permute-start.11 = (bf16[128,1024]{1,0:T(8,128)(2,1)}, bf16[128,1024]{1,0:T(8,128)(2,1)S(1)}, u32[]{:S(2)}, u32[]{:S(2)}) collective-permute-start(bf16[128,1024]{1,0:T(8,128)(2,1)} %refs_3_.1), channel_id=1, source_target_pairs={{0,16},{16,0},{1,17},{17,1},{2,18},{18,2},{3,19},{19,3},{4,20},{20... | collective-permute-start | bytes 786440 | tf_op jit(solution)/shard_map/ppermute | solution.py:902
  3.2 12.9 %collective-permute-start.14 = (bf16[128,1024]{1,0:T(8,128)(2,1)}, bf16[128,1024]{1,0:T(8,128)(2,1)S(1)}, u32[]{:S(2)}, u32[]{:S(2)}) collective-permute-start(bf16[128,1024]{1,0:T(8,128)(2,1)} %refs_3_.1), channel_id=1, source_target_pairs={{0,4},{4,0},{1,5},{5,1},{2,6},{6,2},{3,7},{7,3},{8,12},{12,8},{9,1... | collective-permute-start | bytes 786440 | tf_op jit(solution)/shard_map/ppermute | solution.py:880
  7.6 38.5 %collective-permute-start.4 = (bf16[128,1536]{1,0:T(8,128)(2,1)}, bf16[128,1536]{1,0:T(8,128)(2,1)}, u32[]{:S(2)}, u32[]{:S(2)}) collective-permute-start(bf16[128,1536]{1,0:T(8,128)(2,1)} %copy.34), channel_id=1, source_target_pairs={{0,4},{4,0},{1,5},{5,1},{2,6},{6,2},{3,7},{7,3},{8,12},{12,8},{9,1... | collective-permute-start | bytes 1179656 | tf_op jit(solution)/shard_map/ppermute | solution.py:880
  8.7 37.5 %collective-permute-start = (bf16[256,1024]{1,0:T(8,128)(2,1)}, bf16[256,1024]{1,0:T(8,128)(2,1)S(1)}, u32[]{:S(2)}, u32[]{:S(2)}) collective-permute-start(bf16[256,1024]{1,0:T(8,128)(2,1)} %get-tuple-element.110), channel_id=1, source_target_pairs={{0,0},{1,1},{2,4},{3,5},{4,2},{5,3},{6,6},{7,7},{8,8},{9,9},{10,12... | collective-permute-start | bytes 1572872 | tf_op jit(solution)/shard_map/ppermute | solution.py:891
  15.7 32.0 %collective-permute-start.1 = (bf16[256,1024]{1,0:T(8,128)(2,1)}, bf16[256,1024]{1,0:T(8,128)(2,1)S(1)}, u32[]{:S(2)}, u32[]{:S(2)}) collective-permute-start(bf16[256,1024]{1,0:T(8,128)(2,1)} %get-tuple-element.109), channel_id=1, source_target_pairs={{0,1},{1,0},{2,5},{3,4},{4,3},{5,2},{6,7},{7,6},{8,9},{9,8},{10,13... | collective-permute-start | bytes 1572872 | tf_op jit(solution)/shard_map/ppermute | solution.py:891
  16.1 55.6 %collective-permute-start.19 = (bf16[128,4096]{1,0:T(8,128)(2,1)}, bf16[128,4096]{1,0:T(8,128)(2,1)}, u32[]{:S(2)}, u32[]{:S(2)}) collective-permute-start(bf16[128,4096]{1,0:T(8,128)(2,1)} %refs_2_.1), channel_id=1, source_target_pairs={{0,8},{8,0},{1,9},{9,1},{2,10},{10,2},{3,11},{11,3},{4,12},{12,4},... | collective-permute-start | bytes 3145736 | tf_op jit(solution)/shard_map/ppermute | solution.py:901
  20.1 22.8 %collective-permute-start.13 = (bf16[64,1024]{1,0:T(8,128)(2,1)S(1)}, bf16[64,1024]{1,0:T(8,128)(2,1)S(1)}, u32[]{:S(2)}, u32[]{:S(2)}) collective-permute-start(bf16[64,1024]{1,0:T(8,128)(2,1)S(1)} %slice.214), channel_id=1, source_target_pairs={{0,8},{8,0},{1,9},{9,1},{2,10},{10,2},{3,11},{11,3},{4,12},{12,4},... | collective-permute-start | bytes 393224 | tf_op jit(solution)/shard_map/ppermute | solution.py:905
  42.9 16.5 %collective-permute-start.34 = (bf16[256,1024]{1,0:T(8,128)(2,1)}, bf16[256,1024]{1,0:T(8,128)(2,1)S(1)}, u32[]{:S(2)}, u32[]{:S(2)}) collective-permute-start(bf16[256,1024]{1,0:T(8,128)(2,1)} %get-tuple-element.108), channel_id=1, source_target_pairs={{0,0},{1,1},{2,4},{3,5},{4,2},{5,3},{6,6},{7,7},{8,8},{9,9},{10,12... | collective-permute-start | bytes 1572872 | tf_op jit(solution)/shard_map/ppermute | solution.py:891
  47.7 24.1 %collective-permute-start.35 = (bf16[256,1024]{1,0:T(8,128)(2,1)}, bf16[256,1024]{1,0:T(8,128)(2,1)S(1)}, u32[]{:S(2)}, u32[]{:S(2)}) collective-permute-start(bf16[256,1024]{1,0:T(8,128)(2,1)} %get-tuple-element.107), channel_id=1, source_target_pairs={{0,1},{1,0},{2,5},{3,4},{4,3},{5,2},{6,7},{7,6},{8,9},{9,8},{10,13... | collective-permute-start | bytes 1572872 | tf_op jit(solution)/shard_map/ppermute | solution.py:891
  51.4 24.9 %collective-permute-start.20 = (bf16[128,4096]{1,0:T(8,128)(2,1)}, bf16[128,4096]{1,0:T(8,128)(2,1)}, u32[]{:S(2)}, u32[]{:S(2)}) collective-permute-start(bf16[128,4096]{1,0:T(8,128)(2,1)} %refs_2_.1), channel_id=1, source_target_pairs={{0,16},{16,0},{1,17},{17,1},{2,18},{18,2},{3,19},{19,3},{4,20},{20... | collective-permute-start | bytes 3145736 | tf_op jit(solution)/shard_map/ppermute | solution.py:902
  53.5 67.9 %collective-permute-start.28 = (bf16[512,1024]{1,0:T(8,128)(2,1)}, bf16[512,1024]{1,0:T(8,128)(2,1)}, u32[]{:S(2)}, u32[]{:S(2)}) collective-permute-start(bf16[512,1024]{1,0:T(8,128)(2,1)} %refs_6_.1), channel_id=1, source_target_pairs={{0,8},{8,0},{1,9},{9,1},{2,10},{10,2},{3,11},{11,3},{4,12},{12,4},... | collective-permute-start | bytes 3145736 | tf_op jit(solution)/shard_map/ppermute | solution.py:901
  59.3 63.4 %collective-permute-start.30 = (bf16[512,1024]{1,0:T(8,128)(2,1)}, bf16[512,1024]{1,0:T(8,128)(2,1)}, u32[]{:S(2)}, u32[]{:S(2)}) collective-permute-start(bf16[512,1024]{1,0:T(8,128)(2,1)} %refs_6_.1), channel_id=1, source_target_pairs={{0,16},{16,0},{1,17},{17,1},{2,18},{18,2},{3,19},{19,3},{4,20},{20... | collective-permute-start | bytes 3145736 | tf_op jit(solution)/shard_map/ppermute | solution.py:902
  71.7 23.1 %collective-permute-start.5 = (bf16[256,1536]{1,0:T(8,128)(2,1)S(1)}, bf16[256,1536]{1,0:T(8,128)(2,1)}, u32[]{:S(2)}, u32[]{:S(2)}) collective-permute-start(bf16[256,1536]{1,0:T(8,128)(2,1)S(1)} %pad_maximum_fusion.2.w0), channel_id=1, source_target_pairs={{0,8},{8,0},{1,9},{9,1},{2,10},{10,2},{3,11},{11,3},{4,12},{12,4},... | collective-permute-start | bytes 2359304 | tf_op jit(solution)/shard_map/ppermute | solution.py:901
  71.8 43.9 %collective-permute-start.6 = (bf16[256,1536]{1,0:T(8,128)(2,1)S(1)}, bf16[256,1536]{1,0:T(8,128)(2,1)}, u32[]{:S(2)}, u32[]{:S(2)}) collective-permute-start(bf16[256,1536]{1,0:T(8,128)(2,1)S(1)} %pad_maximum_fusion.2.w0), channel_id=1, source_target_pairs={{0,16},{16,0},{1,17},{17,1},{2,18},{18,2},{3,19},{19,3},{4,20},{20... | collective-permute-start | bytes 2359304 | tf_op jit(solution)/shard_map/ppermute | solution.py:902
  76.3 85.1 %collective-permute-start.23 = (bf16[128,4096]{1,0:T(8,128)(2,1)}, bf16[128,4096]{1,0:T(8,128)(2,1)}, u32[]{:S(2)}, u32[]{:S(2)}) collective-permute-start(bf16[128,4096]{1,0:T(8,128)(2,1)} %refs_2_.1), channel_id=1, source_target_pairs={{0,4},{4,0},{1,5},{5,1},{2,6},{6,2},{3,7},{7,3},{8,12},{12,8},{9,1... | collective-permute-start | bytes 3145736 | tf_op jit(solution)/shard_map/ppermute | solution.py:880
  94.8 33.3 %collective-permute-start.2 = (bf16[256,1024]{1,0:T(8,128)(2,1)S(1)}, bf16[256,1024]{1,0:T(8,128)(2,1)}, u32[]{:S(2)}, u32[]{:S(2)}) collective-permute-start(bf16[256,1024]{1,0:T(8,128)(2,1)S(1)} %collective-permute-done.m0.refs_13_.x0), channel_id=1, source_target_pairs={{0,4},{4,0},{1,5},{5,1},{2,6},{6,2},{3,7},{7,3},{8,12},{12,8},{9,1... | collective-permute-start | bytes 1572872 | tf_op jit(solution)/shard_map/ppermute | solution.py:880
  128.2 35.0 %collective-permute-start.21 = (bf16[64,4096]{1,0:T(8,128)(2,1)S(1)}, bf16[64,4096]{1,0:T(8,128)(2,1)S(1)}, u32[]{:S(2)}, u32[]{:S(2)}) collective-permute-start(bf16[64,4096]{1,0:T(8,128)(2,1)S(1)} %slice.215), channel_id=1, source_target_pairs={{0,16},{16,0},{1,17},{17,1},{2,18},{18,2},{3,19},{19,3},{4,20},{20... | collective-permute-start | bytes 1572872 | tf_op jit(solution)/shard_map/ppermute | solution.py:904
  128.5 34.8 %collective-permute-start.22 = (bf16[64,4096]{1,0:T(8,128)(2,1)S(1)}, bf16[64,4096]{1,0:T(8,128)(2,1)S(1)}, u32[]{:S(2)}, u32[]{:S(2)}) collective-permute-start(bf16[64,4096]{1,0:T(8,128)(2,1)S(1)} %slice.216), channel_id=1, source_target_pairs={{0,8},{8,0},{1,9},{9,1},{2,10},{10,2},{3,11},{11,3},{4,12},{12,4},... | collective-permute-start | bytes 1572872 | tf_op jit(solution)/shard_map/ppermute | solution.py:905
  132.2 31.4 %collective-permute-start.29 = (bf16[256,1024]{1,0:T(8,128)(2,1)S(1)}, bf16[256,1024]{1,0:T(8,128)(2,1)S(1)}, u32[]{:S(2)}, u32[]{:S(2)}) collective-permute-start(bf16[256,1024]{1,0:T(8,128)(2,1)S(1)} %slice.217), channel_id=1, source_target_pairs={{0,16},{16,0},{1,17},{17,1},{2,18},{18,2},{3,19},{19,3},{4,20},{20... | collective-permute-start | bytes 1572872 | tf_op jit(solution)/shard_map/ppermute | solution.py:904
  133.5 30.3 %collective-permute-start.31 = (bf16[256,1024]{1,0:T(8,128)(2,1)S(1)}, bf16[256,1024]{1,0:T(8,128)(2,1)S(1)}, u32[]{:S(2)}, u32[]{:S(2)}) collective-permute-start(bf16[256,1024]{1,0:T(8,128)(2,1)S(1)} %slice.218), channel_id=1, source_target_pairs={{0,8},{8,0},{1,9},{9,1},{2,10},{10,2},{3,11},{11,3},{4,12},{12,4},... | collective-permute-start | bytes 1572872 | tf_op jit(solution)/shard_map/ppermute | solution.py:905
  164.7 30.7 %collective-permute-start.38 = (bf16[512,1024]{1,0:T(8,128)(2,1)}, bf16[512,1024]{1,0:T(8,128)(2,1)S(1)}, u32[]{:S(2)}, u32[]{:S(2)}) collective-permute-start(bf16[512,1024]{1,0:T(8,128)(2,1)} %refs_6_.1), channel_id=1, source_target_pairs={{0,4},{4,0},{1,5},{5,1},{2,6},{6,2},{3,7},{7,3},{8,12},{12,8},{9,1... | collective-permute-start | bytes 3145736 | tf_op jit(solution)/shard_map/ppermute | solution.py:880
  166.2 38.9 %collective-permute-start.36 = (bf16[512,1024]{1,0:T(8,128)(2,1)}, bf16[512,1024]{1,0:T(8,128)(2,1)S(1)}, u32[]{:S(2)}, u32[]{:S(2)}) collective-permute-start(bf16[512,1024]{1,0:T(8,128)(2,1)} %collective-permute-done.28.refs_6_), channel_id=1, source_target_pairs={{0,4},{4,0},{1,5},{5,1},{2,6},{6,2},{3,7},{7,3},{8,12},{12,8},{9,1... | collective-permute-start | bytes 3145736 | tf_op jit(solution)/shard_map/ppermute | solution.py:880
  168.5 36.6 %collective-permute-start.37 = (bf16[512,1024]{1,0:T(8,128)(2,1)}, bf16[512,1024]{1,0:T(8,128)(2,1)S(1)}, u32[]{:S(2)}, u32[]{:S(2)}) collective-permute-start(bf16[512,1024]{1,0:T(8,128)(2,1)} %collective-permute-done.30.refs_8_), channel_id=1, source_target_pairs={{0,4},{4,0},{1,5},{5,1},{2,6},{6,2},{3,7},{7,3},{8,12},{12,8},{9,1... | collective-permute-start | bytes 3145736 | tf_op jit(solution)/shard_map/ppermute | solution.py:880
  168.8 51.0 %collective-permute-start.32 = (bf16[256,1024]{1,0:T(8,128)(2,1)S(1)}, bf16[256,1024]{1,0:T(8,128)(2,1)S(1)}, u32[]{:S(2)}, u32[]{:S(2)}) collective-permute-start(bf16[256,1024]{1,0:T(8,128)(2,1)S(1)} %collective-permute-done.29.wt0), channel_id=1, source_target_pairs={{0,4},{4,0},{1,5},{5,1},{2,6},{6,2},{3,7},{7,3},{8,12},{12,8},{9,1... | collective-permute-start | bytes 1572872 | tf_op jit(solution)/shard_map/ppermute | solution.py:880
  169.4 50.5 %collective-permute-start.33 = (bf16[256,1024]{1,0:T(8,128)(2,1)S(1)}, bf16[256,1024]{1,0:T(8,128)(2,1)S(1)}, u32[]{:S(2)}, u32[]{:S(2)}) collective-permute-start(bf16[256,1024]{1,0:T(8,128)(2,1)S(1)} %collective-permute-done.31.wl0), channel_id=1, source_target_pairs={{0,4},{4,0},{1,5},{5,1},{2,6},{6,2},{3,7},{7,3},{8,12},{12,8},{9,1... | collective-permute-start | bytes 1572872 | tf_op jit(solution)/shard_map/ppermute | solution.py:880
  270.7 31.7 %collective-permute-start.42 = (bf16[512,1024]{1,0:T(8,128)(2,1)}, bf16[512,1024]{1,0:T(8,128)(2,1)S(1)}, u32[]{:S(2)}, u32[]{:S(2)}) collective-permute-start(bf16[512,1024]{1,0:T(8,128)(2,1)} %copy-done.61), channel_id=1, source_target_pairs={{0,4},{4,0},{1,5},{5,1},{2,6},{6,2},{3,7},{7,3},{8,12},{12,8},{9,1... | collective-permute-start | bytes 3145736 | tf_op jit(solution)/shard_map/ppermute | solution.py:880
  283.6 26.4 %collective-permute-start.49 = (f32[4,4,1024]{2,1,0:T(4,128)S(1)}, f32[4,4,1024]{2,1,0:T(4,128)S(1)}, u32[]{:S(2)}, u32[]{:S(2)}) collective-permute-start(f32[4,4,1024]{2,1,0:T(4,128)S(1)} %add.43), channel_id=1, source_target_pairs={{0,2},{2,0},{1,3},{3,1},{4,6},{6,4},{5,7},{7,5},{8,10},{10,8},{9,1... | collective-permute-start | bytes 196616 | tf_op jit(solution)/shard_map/ppermute | solution.py:1017
  296.5 18.5 %collective-permute-start.39 = (bf16[256,1024]{1,0:T(8,128)(2,1)}, bf16[256,1024]{1,0:T(8,128)(2,1)S(1)}, u32[]{:S(2)}, u32[]{:S(2)}) collective-permute-start(bf16[256,1024]{1,0:T(8,128)(2,1)} %get-tuple-element.77), channel_id=1, source_target_pairs={{0,0},{1,1},{2,4},{3,5},{4,2},{5,3},{6,6},{7,7},{8,8},{9,9},{10,12... | collective-permute-start | bytes 1572872 | tf_op jit(solution)/shard_map/ppermute | solution.py:891
  302.3 35.0 %collective-permute-start.40 = (bf16[256,1024]{1,0:T(8,128)(2,1)}, bf16[256,1024]{1,0:T(8,128)(2,1)S(1)}, u32[]{:S(2)}, u32[]{:S(2)}) collective-permute-start(bf16[256,1024]{1,0:T(8,128)(2,1)} %get-tuple-element.78), channel_id=1, source_target_pairs={{0,1},{1,0},{2,5},{3,4},{4,3},{5,2},{6,7},{7,6},{8,9},{9,8},{10,13... | collective-permute-start | bytes 1572872 | tf_op jit(solution)/shard_map/ppermute | solution.py:891
  304.6 37.7 %collective-permute-start.43 = (bf16[256,1024]{1,0:T(8,128)(2,1)S(1)}, bf16[256,1024]{1,0:T(8,128)(2,1)S(1)}, u32[]{:S(2)}, u32[]{:S(2)}) collective-permute-start(bf16[256,1024]{1,0:T(8,128)(2,1)S(1)} %get-tuple-element.93), channel_id=1, source_target_pairs={{0,0},{1,1},{2,4},{3,5},{4,2},{5,3},{6,6},{7,7},{8,8},{9,9},{10,12... | collective-permute-start | bytes 1572872 | tf_op jit(solution)/shard_map/ppermute | solution.py:891
  309.9 38.6 %collective-permute-start.44 = (bf16[256,1024]{1,0:T(8,128)(2,1)S(1)}, bf16[256,1024]{1,0:T(8,128)(2,1)S(1)}, u32[]{:S(2)}, u32[]{:S(2)}) collective-permute-start(bf16[256,1024]{1,0:T(8,128)(2,1)S(1)} %get-tuple-element.94), channel_id=1, source_target_pairs={{0,1},{1,0},{2,5},{3,4},{4,3},{5,2},{6,7},{7,6},{8,9},{9,8},{10,13... | collective-permute-start | bytes 1572872 | tf_op jit(solution)/shard_map/ppermute | solution.py:891
  (93 other events, 1314.5 us)

commit v2 on v1

--- a/solution.py
+++ b/solution.py
@@ -291,6 +291,7 @@
 
 HALF = 512
 BLOCK = 256
+VMEM_MIB = 63
 SMEM = pl.BlockSpec(memory_space=pltpu.SMEM)
 VMEM = pl.BlockSpec(memory_space=pltpu.VMEM)
 HBM = pl.BlockSpec(memory_space=pl.ANY)
@@ -317,8 +318,8 @@
     return jax.ShapeDtypeStruct(dims, dtype)
 
 
-def params(mib):
-    return pltpu.CompilerParams(vmem_limit_bytes=mib * 2**20)
+def params():
+    return pltpu.CompilerParams(vmem_limit_bytes=VMEM_MIB * 2**20)
 
 
 def rows(index, size):
@@ -360,81 +361,118 @@
     return inverse * (grad - first - hat * second)
 
 
+def norm_kernel(ids, m0, m1, gain, shift, out, xs, sems):
+    z = ids[1]
+    go = Copies(sems)
+    arrive = [go.start(ref, xs.at[parity(z, k)]) for k, ref in enumerate((m0, m1))]
+    wait_all(arrive)
+    for i in range(2):
+        hat, _ = center_scale(xs[i].astype(f32))
+        out[i * BLOCK : (i + 1) * BLOCK] = (hat * gain[0:1] + shift[0:1]).astype(bf16)
+
+
+def call_norm(ids, x_own, gain, shift):
+    return pl.pallas_call(
+        norm_kernel,
+        out_shape=shape(HALF, 1024),
+        in_specs=[SMEM, HBM, HBM, VMEM, VMEM],
+        out_specs=VMEM,
+        scratch_shapes=[pltpu.VMEM((2, BLOCK, 1024), bf16), pltpu.SemaphoreType.DMA((2,))],
+        compiler_params=params(),
+        name="norm",
+    )(ids, *x_own, gain, shift)
+
+
+def start_sides(go, piece, target, chip, core, tag):
+    return [
+        (tag, go.start(piece.at[:128], target.at[rows(2 * chip + core, 128)])),
+        (tag, go.start(piece.at[128:], target.at[rows(2 * chip + 1 - core, 128)])),
+    ]
+
+
 def qkv_kernel(
-    ids, m0, m1, o0, o1, w0, w1, w2, w3t, w3b, gain, shift, down_w, up_w, bias,
-    q_out, k_out, v_out, n_out, down_out, w_out, xs, ws, sems,
+    ids, n_own, n_other, w0, w1, w2, w3t, w3b, down_w, up_w, bias,
+    q_out, k_out, v_out, down_out, w_out, o_out, ns, ws, os, outs, downs, sems,
 ):
-    core, z, chip = ids[0], ids[1], ids[2]
+    core, chip = ids[0], ids[2]
     go = Copies(sems)
     arrive = [
-        go.start(ref, xs.at[rows(2 * side + parity(z, k), BLOCK)])
-        for side, pair in ((core, (m0, m1)), (1 - core, (o0, o1)))
-        for k, ref in enumerate(pair)
+        go.start(n_own, ns.at[rows(core, HALF)]),
+        go.start(n_other, ns.at[rows(1 - core, HALF)]),
     ]
-    weights = [
-        go.start(ref, ws.at[rows(chip ^ r, BLOCK)]) for r, ref in enumerate((w0, w1, w2))
-    ]
-    weights.append(go.start(w3t, ws.at[rows(2 * (chip ^ 3), BLOCK // 2)]))
-    weights.append(go.start(w3b, ws.at[rows(2 * (chip ^ 3) + 1, BLOCK // 2)]))
+    weights, outer, passing = [], [], []
+    for r, ref in enumerate((w0, w1, w2, (w3t, w3b))):
+        part = (lambda p: ref.at[p]) if r < 3 else (lambda p: ref[p // 2].at[p % 2])
+        for p in range(3):
+            weights += start_sides(go, part(p), ws.at[p], chip ^ r, core, p)
+        for h in range(2):
+            outer.append(
+                go.start(
+                    part(3).at[h * 128 : (h + 1) * 128],
+                    os.at[rows(chip ^ r, 128), h * HALF : (h + 1) * HALF],
+                )
+            )
     wait_all(arrive)
-
-    @pl.loop(0, 4)
-    def _(i):
-        at = rows(i, BLOCK)
-        hat, _ = center_scale(xs[at].astype(f32))
-        n_out[at] = (hat * gain[...] + shift[...]).astype(bf16)
-
-    wait_all(weights)
-    keep = go.start(ws, w_out)
-
-    @pl.loop(0, 4)
-    def _(i):
-        at = rows(i, BLOCK)
-        n = n_out[at]
-        down = nt(n, down_w[...]).astype(bf16)
-        down_out[at] = down
-        for part, out in enumerate((q_out, k_out, v_out)):
-            cols = slice(part * HALF, (part + 1) * HALF)
-            value = nn(n, ws[:, cols]) + bias[:, cols]
-            if part != 1:
-                value += nn(down, up_w[:, cols])
+    for p, out in enumerate((q_out, k_out, v_out)):
+        wait_all([copy for at, copy in weights if at == p])
+        passing.append(go.start(ws.at[p], w_out.at[p]))
+        for i in range(4):
+            at = slice(i * BLOCK, (i + 1) * BLOCK)
+            if p == 0:
+                downs[at] = nt(ns[at], down_w[...]).astype(bf16)
+            value = nn(ns[at], ws[p]) + bias[:, p * HALF : (p + 1) * HALF]
+            if p != 1:
+                value += nn(downs[at], up_w[:, p * HALF : (p + 1) * HALF])
             value = value.astype(bf16)
-            if part == 0:
+            if p == 0:
                 value = value * jnp.asarray(0.125, bf16)
-            out[at] = value
-
-    keep.wait()
-
-
-def call_qkv(ids, x_own, x_other, pieces, gain, shift, down_w, up_w, bias):
+            outs[p, at] = value
+        passing.append(go.start(outs.at[p], out))
+    passing.append(go.start(downs, down_out))
+    wait_all(outer)
+    passing.append(go.start(os, o_out))
+    wait_all(passing)
+
+
+def call_qkv(ids, n_own, n_other, pieces, down_w, up_w, bias):
     return pl.pallas_call(
         qkv_kernel,
         out_shape=(
             shape(1024, HALF),
             shape(1024, HALF),
             shape(1024, HALF),
-            shape(1024, 1024),
             shape(1024, 128),
-            shape(1024, 1536),
+            shape(3, 1024, HALF),
+            shape(HALF, 1024),
         ),
-        in_specs=[SMEM] + [HBM] * 9 + [VMEM] * 5,
-        out_specs=(VMEM,) * 5 + (HBM,),
+        in_specs=[SMEM] + [HBM] * 7 + [VMEM] * 3,
+        out_specs=(HBM,) * 6,
         scratch_shapes=[
             pltpu.VMEM((1024, 1024), bf16),
-            pltpu.VMEM((1024, 1536), bf16),
-            pltpu.SemaphoreType.DMA((10,)),
+            pltpu.VMEM((3, 1024, HALF), bf16),
+            pltpu.VMEM((HALF, 1024), bf16),
+            pltpu.VMEM((3, 1024, HALF), bf16),
+            pltpu.VMEM((1024, 128), bf16),
+            pltpu.SemaphoreType.DMA((42,)),
         ],
-        compiler_params=params(40),
+        compiler_params=params(),
         name="qkv",
-    )(ids, *x_own, *x_other, *pieces, gain, shift, down_w, up_w, bias)
+    )(ids, n_own, n_other, *pieces, down_w, up_w, bias)
 
 
 def low_half(value):
     return lax.broadcasted_iota(jnp.int32, value.shape, 1) < 64
 
 
-def forward_kernel(ids, q, k, v, ctx, stat, send):
+def forward_kernel(ids, q, k, v, w_o, ctx, stat, own, send, ctxs, wos, sems):
     core = ids[0]
+    pair = pl.program_id(0)
+    copy = pltpu.make_async_copy(w_o, wos, sems.at[0])
+
+    @pl.when(pair == 0)
+    def _():
+        copy.start()
+
     keys = k[...]
     values = v[...]
     low = low_half(values)
@@ -461,34 +499,68 @@
         wide = low_half(heads[0])
         sums = jnp.where(wide, heads[1], heads[0])
         sums = pltpu.roll(sums, 64, 1)
-        ctx[i * BLOCK : ext] = (jnp.where(wide, heads[0], heads[1]) / sums).astype(bf16)
+        value = (jnp.where(wide, heads[0], heads[1]) / sums).astype(bf16)
+        ctx[i * BLOCK : ext] = value
+        ctxs[pair, i * BLOCK : ext] = value
         total = jnp.where(wide, tops[0], tops[1]) + jnp.log(sums)
         total = jnp.transpose(total)
         stat[0, :, i * BLOCK : ext] = jnp.concatenate([total[0:1], total[64:65]] * 4, axis=0)
-    send[...] = ctx[rows(1 - core, HALF)]
-
-
-def call_forward(ids, q, k, v):
+
+    @pl.when(pair == 3)
+    def _():
+        copy.wait()
+        for side, out in ((1 - core, send), (core, own)):
+            for i in range(2):
+                at = rows(2 * side + i, BLOCK)
+                whole = jnp.concatenate([ctxs[p, at] for p in range(4)], axis=1)
+                out[i * BLOCK : (i + 1) * BLOCK] = nn(whole, wos[...]).astype(out.dtype)
+
+
+def call_forward(ids, q, k, v, w_o):
     pair = pl.BlockSpec((1024, 128), lambda p: (0, p))
     return pl.pallas_call(
         forward_kernel,
         grid=(4,),
-        out_shape=(shape(1024, HALF), shape(4, 8, 1024, dtype=f32), shape(HALF, HALF)),
-        in_specs=[SMEM, pair, pair, pair],
+        out_shape=(
+            shape(1024, HALF),
+            shape(4, 8, 1024, dtype=f32),
+            shape(HALF, 1024, dtype=f32),
+            shape(HALF, 1024),
+        ),
+        in_specs=[SMEM, pair, pair, pair, HBM],
         out_specs=(
             pair,
             pl.BlockSpec((1, 8, 1024), lambda p: (p, 0, 0)),
-            pl.BlockSpec((HALF, 128), lambda p: (0, p)),
+            pl.BlockSpec((HALF, 1024), lambda p: (0, 0)),
+            pl.BlockSpec((HALF, 1024), lambda p: (0, 0)),
         ),
-        compiler_params=params(40),
+        scratch_shapes=[
+            pltpu.VMEM((4, 1024, 128), bf16),
+            pltpu.VMEM((HALF, 1024), bf16),
+            pltpu.SemaphoreType.DMA((1,)),
+        ],
+        compiler_params=params(),
         name="attention",
-    )(ids, q, k, v)
-
-
-def backward_kernel(ids, q, k, v, ctx, stat, g_own, g_other, dq, dk, dv, grads, acc_k, acc_v):
+    )(ids, q, k, v, w_o)
+
+
+def backward_kernel(
+    ids, q, k, v, ctx, stat, w_o, g_own, g_other, dq, dk, dv, grads, acc_k, acc_v, gs, sems
+):
     core = ids[0]
-    grads[rows(core, HALF)] = g_own[...]
-    grads[rows(1 - core, HALF)] = g_other[...]
+
+    @pl.when(pl.program_id(0) == 0)
+    def _():
+        go = Copies(sems)
+        arrive = [
+            go.start(g_own, gs.at[rows(core, HALF)]),
+            go.start(g_other, gs.at[rows(1 - core, HALF)]),
+        ]
+        wait_all(arrive)
+
+    for i in range(4):
+        at = slice(i * BLOCK, (i + 1) * BLOCK)
+        grads[at] = nt(gs[at], w_o[...]).astype(bf16)
     keys = k[...]
     values = v[...]
     product = grads[...].astype(f32) * ctx[...].astype(f32)
@@ -531,315 +603,423 @@
     dv[...] = acc_v[...].astype(bf16)
 
 
-def call_backward(ids, q, k, v, ctx, stat, g_own, g_other):
+def call_backward(ids, q, k, v, ctx, stat, w_o, g_own, g_other):
     pair = pl.BlockSpec((1024, 128), lambda p: (0, p))
-    half = pl.BlockSpec((HALF, 128), lambda p: (0, p))
     return pl.pallas_call(
         backward_kernel,
         grid=(4,),
         out_shape=(shape(1024, HALF),) * 3,
-        in_specs=[SMEM, pair, pair, pair, pair, pl.BlockSpec((1, 8, 1024), lambda p: (p, 0, 0)), half, half],
+        in_specs=[
+            SMEM,
+            pair,
+            pair,
+            pair,
+            pair,
+            pl.BlockSpec((1, 8, 1024), lambda p: (p, 0, 0)),
+            pl.BlockSpec((128, 1024), lambda p: (p, 0)),
+            HBM,
+            HBM,
+        ],
         out_specs=(pair,) * 3,
         scratch_shapes=[
             pltpu.VMEM((1024, 128), bf16),
             pltpu.VMEM((1024, 128), f32),
             pltpu.VMEM((1024, 128), f32),
+            pltpu.VMEM((1024, 1024), bf16),
+            pltpu.SemaphoreType.DMA((2,)),
         ],
-        compiler_params=params(40),
+        compiler_params=params(),
         name="attention_back",
-    )(ids, q, k, v, ctx, stat, g_own, g_other)
-
-
-def start_pieces(go, pieces, target, chip, size):
-    own, by_x, by_y, top, low = pieces
-    return [
-        go.start(own, target.at[rows(chip, size)]),
-        go.start(by_x, target.at[rows(chip ^ 1, size)]),
-        go.start(by_y, target.at[rows(chip ^ 2, size)]),
-        go.start(top, target.at[rows(2 * (chip ^ 3), size // 2)]),
-        go.start(low, target.at[rows(2 * (chip ^ 3) + 1, size // 2)]),
-    ]
+    )(ids, q, k, v, ctx, stat, w_o, g_own, g_other)
 
 
 def start_tokens(go, pair, target, z):
-    return [go.start(ref, target.at[rows(parity(z, k), BLOCK)]) for k, ref in enumerate(pair)]
-
-
-def middle_kernel(*refs):
-    ids, ctx, other = refs[:3]
-    mine, theirs = refs[3:8], refs[8:13]
-    x0, x1, bias, gain, shift, middle, normed, w_out, cs, ws, xs, sems = refs[13:]
-    core, z, chip = ids[0], ids[1], ids[2]
+    return [go.start(ref, target.at[parity(z, k)]) for k, ref in enumerate(pair)]
+
+
+def middle_kernel(
+    ids, own, other, x0, x1, bias, gain, shift, middle, normed, owns, others, xs, mids, ns, sems
+):
     go = Copies(sems)
-    arrive = [go.start(ctx.at[rows(core, HALF)], cs)]
-    arrive += start_pieces(go, mine, ws.at[0], chip, 128)
-    arrive += start_pieces(go, theirs, ws.at[1], chip, 128)
-    arrive += start_tokens(go, (x0, x1), xs, z)
-    wait_all(arrive)
-    keep = go.start(ws, w_out)
-
-    @pl.loop(0, 2)
-    def _(i):
-        at = rows(i, BLOCK)
-        value = nn(cs[at], ws[0]) + nn(other[at], ws[1])
-        value = value + xs[at].astype(f32) + bias[...]
-        middle[at] = value
+    tokens = start_tokens(go, (x0, x1), xs, ids[1])
+    parts = []
+    for i in range(2):
+        at = slice(i * BLOCK, (i + 1) * BLOCK)
+        parts.append([go.start(own.at[at], owns.at[i]), go.start(other.at[at], others.at[i])])
+    wait_all(tokens)
+    leave = []
+    for i in range(2):
+        at = slice(i * BLOCK, (i + 1) * BLOCK)
+        wait_all(parts[i])
+        value = owns[i] + others[i].astype(f32) + xs[i].astype(f32) + bias[2:3]
+        mids[i] = value
+        leave.append(go.start(mids.at[i], middle.at[at]))
         hat, _ = center_scale(value)
-        normed[at] = (hat * gain[...] + shift[...]).astype(bf16)
-
-    keep.wait()
-
-
-def call_middle(ids, ctx, other, mine, theirs, x_own, bias, gain, shift):
+        ns[i] = (hat * gain[1:2] + shift[1:2]).astype(bf16)
+        leave.append(go.start(ns.at[i], normed.at[at]))
+    wait_all(leave)
+
+
+def call_middle(ids, own, other, x_own, bias, gain, shift):
     return pl.pallas_call(
         middle_kernel,
-        out_shape=(shape(HALF, 1024, dtype=f32), shape(HALF, 1024), shape(2, HALF, 1024)),
-        in_specs=[SMEM, HBM, VMEM] + [HBM] * 12 + [VMEM] * 3,
-        out_specs=(VMEM, VMEM, HBM),
+        out_shape=(shape(HALF, 1024, dtype=f32), shape(HALF, 1024)),
+        in_specs=[SMEM] + [HBM] * 4 + [VMEM] * 3,
+        out_specs=(HBM, HBM),
         scratch_shapes=[
-            pltpu.VMEM((HALF, HALF), bf16),
-            pltpu.VMEM((2, HALF, 1024), bf16),
-            pltpu.VMEM((HALF, 1024), bf16),
-            pltpu.SemaphoreType.DMA((14,)),
+            pltpu.VMEM((2, BLOCK, 1024), f32),
+            pltpu.VMEM((2, BLOCK, 1024), bf16),
+            pltpu.VMEM((2, BLOCK, 1024), bf16),
+            pltpu.VMEM((2, BLOCK, 1024), f32),
+            pltpu.VMEM((2, BLOCK, 1024), bf16),
+            pltpu.SemaphoreType.DMA((10,)),
         ],
-        compiler_params=params(32),
+        compiler_params=params(),
         name="middle",
-    )(ids, ctx, other, *mine, *theirs, *x_own, bias, gain, shift)
-
-
-def hidden_kernel(*refs):
-    ids, normed = refs[:2]
-    mine, theirs = refs[2:7], refs[7:12]
-    bias, active, slope, w_out, ws, sems = refs[12:]
+    )(ids, own, other, *x_own, bias, gain, shift)
+
+
+def hidden_kernel(
+    ids, n_own, n_other, w0, w1, w2, w3t, w3b, bias,
+    active, slope, w_out, ns, ws, acts, slopes, sems,
+):
     core, chip = ids[0], ids[2]
     go = Copies(sems)
-    arrive = []
-    for side, pieces in ((core, mine), (1 - core, theirs)):
-        own, by_x, by_y, top, low = pieces
-        for r, ref in enumerate((own, by_x, by_y)):
-            arrive.append(go.start(ref, ws.at[rows(2 * (chip ^ r) + side, 128)]))
-        arrive.append(go.start(top, ws.at[rows(4 * (chip ^ 3) + 2 * side, 64)]))
-        arrive.append(go.start(low, ws.at[rows(4 * (chip ^ 3) + 2 * side + 1, 64)]))
+    arrive = [
+        go.start(n_own, ns.at[rows(core, HALF)]),
+        go.start(n_other, ns.at[rows(1 - core, HALF)]),
+    ]
+    weights = []
+    for r, ref in enumerate((w0, w1, w2, (w3t, w3b))):
+        for p in range(4):
+            part = ref.at[p] if r < 3 else ref[p // 2].at[p % 2]
+            weights += start_sides(go, part, ws.at[p], chip ^ r, core, p)
     wait_all(arrive)
-    keep = [go.start(ws.at[:, d * HALF : (d + 1) * HALF], w_out.at[d]) for d in range(8)]
-    for d in range(8):
-        cols = slice(d * HALF, (d + 1) * HALF)
-
-        @pl.loop(0, 2)
-        def _(i):
-            at = rows(i, BLOCK)
-            h = nn(normed[at], ws[:, cols]) + bias[:, cols]
+    leave = []
+    for p in range(4):
+        wait_all([copy for at, copy in weights if at == p])
+        leave.append(go.start(ws.at[p], w_out.at[p]))
+        shift = bias[pl.ds(2 * p + core, 1)]
+        for i in range(4):
+            at = slice(i * BLOCK, (i + 1) * BLOCK)
+            h = nn(ns[at], ws[p]) + shift
             square = h * h
             t = jnp.tanh(h * (GELU_A + (GELU_A * GELU_B) * square))
             lift = 0.5 + 0.5 * t
-            active[d, at] = (h * lift).astype(bf16)
+            acts[p, at] = (h * lift).astype(bf16)
             inner = GELU_A + (3.0 * GELU_A * GELU_B) * square
-            slope[d, at] = (lift + (0.5 * h) * (1.0 - t * t) * inner).astype(bf16)
-
-    wait_all(keep)
-
-
-def call_hidden(ids, normed, mine, theirs, bias):
+            slopes[p, at] = (lift + (0.5 * h) * (1.0 - t * t) * inner).astype(bf16)
+        leave.append(go.start(acts.at[p], active.at[p]))
+        leave.append(go.start(slopes.at[p], slope.at[p]))
+    wait_all(leave)
+
+
+def call_hidden(ids, n_own, n_other, pieces, bias):
     return pl.pallas_call(
         hidden_kernel,
-        out_shape=(shape(8, HALF, HALF), shape(8, HALF, HALF), shape(8, 1024, HALF)),
-        in_specs=[SMEM, VMEM] + [HBM] * 10 + [VMEM],
-        out_specs=(VMEM, VMEM, HBM),
-        scratch_shapes=[pltpu.VMEM((1024, 4096), bf16), pltpu.SemaphoreType.DMA((18,))],
-        compiler_params=params(48),
+        out_shape=(shape(4, 1024, HALF),) * 3,
+        in_specs=[SMEM] + [HBM] * 7 + [VMEM],
+        out_specs=(HBM,) * 3,
+        scratch_shapes=[pltpu.VMEM((1024, 1024), bf16)]
+        + [pltpu.VMEM((4, 1024, HALF), bf16)] * 3
+        + [pltpu.SemaphoreType.DMA((46,))],
+        compiler_params=params(),
         name="hidden",
-    )(ids, normed, *mine, *theirs, bias)
+    )(ids, n_own, n_other, *pieces, bias)
+
+
+def start_grads(go, ids, g_own, g_other, gs):
+    core, z = ids[0], ids[1]
+    return [
+        go.start(ref, gs.at[2 * side + parity(z, k)])
+        for side, pair in ((core, g_own), (1 - core, g_other))
+        for k, ref in enumerate(pair)
+    ]
 
 
 def feed_kernel(steps, first, *refs):
     n = len(steps)
-    ids, g0, g1, active, slope, w_in = refs[:6]
-    pieces = refs[6 : 6 + n]
-    refs = refs[6 + n :]
+    ids, g0, g1, g2, g3, active, slope, w_in = refs[:8]
+    pieces, refs = refs[8 : 8 + n], refs[8 + n :]
     if not first:
-        old_result, old_grad, refs = refs[0], refs[1], refs[2:]
-    result, grad, gs, acts, slopes, w_ins, w_outs, sems = refs[:8]
-    core, z, chip = ids[0], ids[1], ids[2]
+        old, refs = refs[:2], refs[2:]
+    result, grad, gs, acts, slopes, w_ins, w_outs, res_acc, grad_acc, sems = refs
+    chip = ids[2]
     go = Copies(sems)
-    tokens = start_tokens(go, (g0, g1), gs, z)
+    tokens = start_grads(go, ids, (g0, g1), (g2, g3), gs)
     copies = []
-    for at, (r, side) in enumerate(steps):
-        d = 2 * (chip ^ r) + (core ^ side)
+    for at, r in enumerate(steps):
         copies.append(
             [
                 go.start(pieces[at], w_outs.at[at]),
-                go.start(slope.at[d], slopes.at[at]),
-                go.start(w_in.at[d], w_ins.at[at]),
-                go.start(active.at[d], acts.at[at]),
+                go.start(slope.at[chip ^ r], slopes.at[at]),
+                go.start(w_in.at[chip ^ r], w_ins.at[at]),
+                go.start(active.at[chip ^ r], acts.at[at]),
             ]
         )
+    if not first:
+        loads = []
+        for i in range(4):
+            tok = slice(i * BLOCK, (i + 1) * BLOCK)
+            loads.append(
+                [
+                    go.start(old[0].at[tok], res_acc.at[tok]),
+                    go.start(old[1].at[tok], grad_acc.at[tok]),
+                ]
+            )
     wait_all(tokens)
     for at in range(n):
         wait_all(copies[at])
-
-        @pl.loop(0, 2)
-        def _(i):
-            tok = rows(i, BLOCK)
-            back = nt(gs[tok], w_outs[at]) * slopes[at, tok].astype(f32)
-            more = nt(back.astype(bf16), w_ins[at])
-            out = nn(acts[at, tok], w_outs[at])
-            if at == 0:
-                if first:
-                    grad[tok] = more
-                    result[tok] = out
-                else:
-                    grad[tok] = old_grad[tok] + more
-                    result[tok] = old_result[tok] + out
-            else:
-                grad[tok] += more
-                result[tok] += out
-
-
-def call_feed(ids, steps, g_own, active, slope, w_in, pieces, old):
+    leave = []
+    for i in range(4):
+        tok = slice(i * BLOCK, (i + 1) * BLOCK)
+        more = out = None
+        for at in range(n):
+            back = nt(gs[i], w_outs[at]) * slopes[at, tok].astype(f32)
+            term = nt(back.astype(bf16), w_ins[at])
+            more = term if more is None else more + term
+            term = nn(acts[at, tok], w_outs[at])
+            out = term if out is None else out + term
+        if not first:
+            wait_all(loads[i])
+            more += grad_acc[tok]
+            out += res_acc[tok]
+        grad_acc[tok] = more
+        res_acc[tok] = out
+        leave.append(go.start(res_acc.at[tok], result.at[tok]))
+        leave.append(go.start(grad_acc.at[tok], grad.at[tok]))
+    wait_all(leave)
+
+
+def call_feed(ids, steps, g_own, g_other, active, slope, w_in, pieces, old=()):
     n = len(steps)
-    first = old is None
     return pl.pallas_call(
-        functools.partial(feed_kernel, steps, first),
-        out_shape=(shape(HALF, 1024, dtype=f32),) * 2,
-        in_specs=[SMEM] + [HBM] * (5 + n) + ([] if first else [VMEM, VMEM]),
-        out_specs=(VMEM, VMEM),
+        functools.partial(feed_kernel, steps, not old),
+        out_shape=(shape(1024, 1024, dtype=f32),) * 2,
+        in_specs=[SMEM] + [HBM] * (7 + n + len(old)),
+        out_specs=(HBM, HBM),
         scratch_shapes=[
-            pltpu.VMEM((HALF, 1024), bf16),
-            pltpu.VMEM((n, HALF, HALF), bf16),
-            pltpu.VMEM((n, HALF, HALF), bf16),
+            pltpu.VMEM((4, BLOCK, 1024), bf16),
+            pltpu.VMEM((n, 1024, HALF), bf16),
+            pltpu.VMEM((n, 1024, HALF), bf16),
             pltpu.VMEM((n, 1024, HALF), bf16),
             pltpu.VMEM((n, HALF, 1024), bf16),
-            pltpu.SemaphoreType.DMA((2 + 4 * n,)),
+            pltpu.VMEM((1024, 1024), f32),
+            pltpu.VMEM((1024, 1024), f32),
+            pltpu.SemaphoreType.DMA((4 + 4 * n + 16,)),
         ],
-        compiler_params=params(48),
+        compiler_params=params(),
         name="feed",
-    )(ids, *g_own, active, slope, w_in, *pieces, *(() if first else old))
-
-
-def last_grad_kernel(
-    ids, g0, g1, slope, w_in, wt0, wl0, wt1, wl1, old_grad, middle, gain, w_o,
-    grad_middle, ctx_own, ctx_send, gs, slopes, w_ins, w_outs, sems,
+    )(ids, *g_own, *g_other, active, slope, w_in, *pieces, *old)
+
+
+def far_send_kernel(
+    ids, g0, g1, slope, w_in, top, low, old, out, gs, slopes, w_ins, w_outs, olds, outs, sems
 ):
     core, z, chip = ids[0], ids[1], ids[2]
     go = Copies(sems)
-    tokens = start_tokens(go, (g0, g1), gs, z)
-    copies = []
-    for at, (top, low) in enumerate(((wt0, wl0), (wt1, wl1))):
-        d = 2 * (chip ^ 3) + (core ^ at)
-        copies.append(
-            [
-                go.start(top, w_outs.at[at, :BLOCK]),
-                go.start(low, w_outs.at[at, BLOCK:]),
-                go.start(slope.at[d], slopes.at[at]),
-                go.start(w_in.at[d], w_ins.at[at]),
-            ]
-        )
-    wait_all(tokens)
-    wait_all(copies[0])
-    wait_all(copies[1])
-
-    @pl.loop(0, 2)
-    def _(i):
-        tok = rows(i, BLOCK)
-        grad = old_grad[tok]
-        for at in range(2):
-            back = nt(gs[tok], w_outs[at]) * slopes[at, tok].astype(f32)
-            grad += nt(back.astype(bf16), w_ins[at])
-        hat, inverse = center_scale(middle[tok])
-        value = gs[tok].astype(f32) + norm_back(hat, inverse, grad * gain[...])
-        grad_middle[tok] = value
-        low_value = value.astype(bf16)
-        ctx_own[tok] = nt(low_value, w_o[0]).astype(bf16)
-        ctx_send[tok] = nt(low_value, w_o[1]).astype(bf16)
-
-
-def call_last_grad(ids, g_own, slope, w_in, halves, old_grad, middle, gain, w_o):
+    arrive = start_tokens(go, (g0, g1), gs, z)
+    arrive.append(go.start(top, w_outs.at[:BLOCK]))
+    arrive.append(go.start(low, w_outs.at[BLOCK:]))
+    arrive.append(go.start(slope.at[chip ^ 3, rows(1 - core, HALF)], slopes))
+    arrive.append(go.start(w_in.at[chip ^ 3], w_ins))
+    load = go.start(old.at[rows(1 - core, HALF)], olds)
+    wait_all(arrive)
+    leave = []
+    for i in range(2):
+        tok = slice(i * BLOCK, (i + 1) * BLOCK)
+        back = nt(gs[i], w_outs[...]) * slopes[tok].astype(f32)
+        more = nt(back.astype(bf16), w_ins[...])
+        if i == 0:
+            load.wait()
+        outs[tok] = (more + olds[tok]).astype(bf16)
+        leave.append(go.start(outs.at[tok], out.at[tok]))
+    wait_all(leave)
+
+
+def call_far_send(ids, g_other, slope, w_in, far, old):
     return pl.pallas_call(
-        last_grad_kernel,
-        out_shape=(shape(HALF, 1024, dtype=f32), shape(HALF, HALF), shape(HALF, HALF)),
-        in_specs=[SMEM] + [HBM] * 8 + [VMEM] * 4,
-        out_specs=(VMEM,) * 3,
+        far_send_kernel,
+        out_shape=shape(HALF, 1024),
+        in_specs=[SMEM] + [HBM] * 7,
+        out_specs=HBM,
         scratch_shapes=[
+            pltpu.VMEM((2, BLOCK, 1024), bf16),
+            pltpu.VMEM((HALF, HALF), bf16),
+            pltpu.VMEM((1024, HALF), bf16),
             pltpu.VMEM((HALF, 1024), bf16),
-            pltpu.VMEM((2, HALF, HALF), bf16),
-            pltpu.VMEM((2, 1024, HALF), bf16),
-            pltpu.VMEM((2, HALF, 1024), bf16),
-            pltpu.SemaphoreType.DMA((10,)),
+            pltpu.VMEM((HALF, 1024), f32),
+            pltpu.VMEM((HALF, 1024), bf16),
+            pltpu.SemaphoreType.DMA((9,)),
         ],
-        compiler_params=params(48),
-        name="middle_grad",
-    )(ids, *g_own, slope, w_in, *halves, old_grad, middle, gain, w_o)
-
-
-def last_result_kernel(
-    ids, active, wt0, wl0, wt1, wl1, old_result, middle, bias, out0, out1, acts, w_outs, sems
+        compiler_params=params(),
+        name="far_send",
+    )(ids, *g_other, slope, w_in, *far, old)
+
+
+def far_own_kernel(
+    ids, g0, g1, slope, w_in, top, low, old, other, middle, gain, grad_out, low_out,
+    gs, slopes, w_ins, w_outs, olds, others, mids, grads, lows, sems,
 ):
     core, z, chip = ids[0], ids[1], ids[2]
     go = Copies(sems)
-    arrive = []
-    for at, (top, low) in enumerate(((wt0, wl0), (wt1, wl1))):
-        d = 2 * (chip ^ 3) + (core ^ at)
-        arrive.append(go.start(top, w_outs.at[at, :BLOCK]))
-        arrive.append(go.start(low, w_outs.at[at, BLOCK:]))
-        arrive.append(go.start(active.at[d], acts.at[at]))
+    arrive = start_tokens(go, (g0, g1), gs, z)
+    arrive.append(go.start(top, w_outs.at[:BLOCK]))
+    arrive.append(go.start(low, w_outs.at[BLOCK:]))
+    arrive.append(go.start(slope.at[chip ^ 3, rows(core, HALF)], slopes))
+    arrive.append(go.start(w_in.at[chip ^ 3], w_ins))
+    loads = [
+        go.start(old.at[rows(core, HALF)], olds),
+        go.start(other, others),
+        go.start(middle, mids),
+    ]
     wait_all(arrive)
+    leave = []
+    for i in range(2):
+        tok = slice(i * BLOCK, (i + 1) * BLOCK)
+        back = nt(gs[i], w_outs[...]) * slopes[tok].astype(f32)
+        more = nt(back.astype(bf16), w_ins[...])
+        if i == 0:
+            wait_all(loads)
+        more += olds[tok] + others[tok].astype(f32)
+        hat, inverse = center_scale(mids[tok])
+        value = gs[i].astype(f32) + norm_back(hat, inverse, more * gain[1:2])
+        grads[tok] = value
+        lows[tok] = value.astype(bf16)
+        leave.append(go.start(grads.at[tok], grad_out.at[tok]))
+        leave.append(go.start(lows.at[tok], low_out.at[tok]))
+    wait_all(leave)
+
+
+def call_far_own(ids, g_own, slope, w_in, far, old, other, middle, gain):
+    return pl.pallas_call(
+        far_own_kernel,
+        out_shape=(shape(HALF, 1024, dtype=f32), shape(HALF, 1024)),
+        in_specs=[SMEM] + [HBM] * 9 + [VMEM],
+        out_specs=(HBM, HBM),
+        scratch_shapes=[
+            pltpu.VMEM((2, BLOCK, 1024), bf16),
+            pltpu.VMEM((HALF, HALF), bf16),
+            pltpu.VMEM((1024, HALF), bf16),
+            pltpu.VMEM((HALF, 1024), bf16),
+            pltpu.VMEM((HALF, 1024), f32),
+            pltpu.VMEM((HALF, 1024), bf16),
+            pltpu.VMEM((HALF, 1024), f32),
+            pltpu.VMEM((HALF, 1024), f32),
+            pltpu.VMEM((HALF, 1024), bf16),
+            pltpu.SemaphoreType.DMA((13,)),
+        ],
+        compiler_params=params(),
+        name="far_own",
+    )(ids, *g_own, slope, w_in, *far, old, other, middle, gain)
+
+
+def far_result_kernel(
+    ids, active, top, low, old, own, send, acts, w_outs, olds, owns, sends, sems
+):
+    core, chip = ids[0], ids[2]
+    go = Copies(sems)
+    arrive = [
+        go.start(top, w_outs.at[:BLOCK]),
+        go.start(low, w_outs.at[BLOCK:]),
+        go.start(active.at[chip ^ 3], acts),
+    ]
+    load = go.start(old, olds)
+    wait_all(arrive)
+    load.wait()
+    leave = []
+    for side, values, out in ((1 - core, sends, send), (core, owns, own)):
+        for i in range(2):
+            at = rows(2 * side + i, BLOCK)
+            tok = slice(i * BLOCK, (i + 1) * BLOCK)
+            values[tok] = (olds[at] + nn(acts[at], w_outs[...])).astype(values.dtype)
+            leave.append(go.start(values.at[tok], out.at[tok]))
+    wait_all(leave)
+
+
+def call_far_result(ids, active, far, old):
+    return pl.pallas_call(
+        far_result_kernel,
+        out_shape=(shape(HALF, 1024, dtype=f32), shape(HALF, 1024)),
+        in_specs=[SMEM] + [HBM] * 4,
+        out_specs=(HBM, HBM),
+        scratch_shapes=[
+            pltpu.VMEM((1024, HALF), bf16),
+            pltpu.VMEM((HALF, 1024), bf16),
+            pltpu.VMEM((1024, 1024), f32),
+            pltpu.VMEM((HALF, 1024), f32),
+            pltpu.VMEM((HALF, 1024), bf16),
+            pltpu.SemaphoreType.DMA((8,)),
+        ],
+        compiler_params=params(),
+        name="far_result",
+    )(ids, active, *far, old)
+
+
+def mixed_kernel(ids, own, other, middle, bias, out0, out1):
+    z = ids[1]
     for k, out in enumerate((out0, out1)):
         tok = rows(parity(z, k), BLOCK)
-        value = old_result[tok] + middle[tok] + bias[...]
-        for at in range(2):
-            value += nn(acts[at, tok], w_outs[at])
+        value = own[tok] + other[tok].astype(f32) + middle[tok] + bias[3:4]
         out[...] = value.astype(bf16)
 
 
-def call_last_result(ids, active, halves, old_result, middle, bias):
+def call_mixed(ids, own, other, middle, bias):
     return pl.pallas_call(
-        last_result_kernel,
+        mixed_kernel,
         out_shape=(shape(BLOCK, 1024),) * 2,
-        in_specs=[SMEM] + [HBM] * 5 + [VMEM] * 3,
-        out_specs=(VMEM,) * 2,
-        scratch_shapes=[
-            pltpu.VMEM((2, HALF, HALF), bf16),
-            pltpu.VMEM((2, HALF, 1024), bf16),
-            pltpu.SemaphoreType.DMA((6,)),
-        ],
-        compiler_params=params(32),
-        name="result",
-    )(ids, active, *halves, old_result, middle, bias)
+        in_specs=[SMEM] + [VMEM] * 4,
+        out_specs=(VMEM, VMEM),
+        compiler_params=params(),
+        name="mixed",
+    )(ids, own, other, middle, bias)
 
 
 def qkv_back_kernel(
-    ids, dq, dk, dv, w, normed, down, down_w, up_w, own, send, g_norm, g_up, tilt_acc, up_acc
+    ids, dq, dk, dv, w, n_own, n_other, down, down_w, up_w, own, send, g_norm, g_up,
+    qs, ks, vs, ws, ns, downs, owns, sends, tilt_acc, up_acc, sems,
 ):
     core = ids[0]
-    tilt_acc[...] = jnp.zeros_like(tilt_acc)
-    up_acc[...] = jnp.zeros_like(up_acc)
-
-    @pl.loop(0, 4)
-    def _(i):
-        at = rows(i, BLOCK)
-        gq, gk, gv = dq[at], dk[at], dv[at]
+    go = Copies(sems)
+    weights = go.start(w, ws)
+    later = [
+        go.start(n_own, ns.at[rows(core, HALF)]),
+        go.start(n_other, ns.at[rows(1 - core, HALF)]),
+        go.start(down, downs),
+    ]
+    order = [2 * side + i for side in (1 - core, core) for i in range(2)]
+    grads = [
+        [go.start(ref.at[rows(i, BLOCK)], to.at[at]) for ref, to in ((dq, qs), (dk, ks), (dv, vs))]
+        for at, i in enumerate(order)
+    ]
+    weights.wait()
+    leave = []
+    for at in range(4):
+        wait_all(grads[at])
+        gq, gk, gv = qs[at], ks[at], vs[at]
         tilt = (nt(gq, up_w[:, :HALF]) + nt(gv, up_w[:, 2 * HALF :])).astype(bf16)
-        value = nt(gq, w[:, :HALF]) + nt(gk, w[:, HALF : 2 * HALF]) + nt(gv, w[:, 2 * HALF :])
-        value = (value + nn(tilt, down_w[...])).astype(bf16)
-        place = rows(lax.rem(i, 2), BLOCK)
-
-        @pl.when(i // 2 == core)
-        def _():
-            own[place] = value
-
-        @pl.when(i // 2 != core)
-        def _():
-            send[place] = value
-
-        tilt_acc[...] += tn(tilt, normed[at])
-        up_acc[:, :HALF] += tn(down[at], gq)
-        up_acc[:, HALF:] += tn(down[at], gv)
-
+        value = nt(gq, ws[0]) + nt(gk, ws[1]) + nt(gv, ws[2]) + nn(tilt, down_w[...])
+        values, out = (sends, send) if at < 2 else (owns, own)
+        tok = slice(at % 2 * BLOCK, (at % 2 + 1) * BLOCK)
+        values[tok] = value.astype(bf16)
+        leave.append(go.start(values.at[tok], out.at[tok]))
+        if at == 0:
+            wait_all(later)
+        here = rows(order[at], BLOCK)
+        tilt_term = tn(tilt, ns[here])
+        up_term = jnp.concatenate([tn(downs[here], gq), tn(downs[here], gv)], axis=1)
+        if at == 0:
+            tilt_acc[...] = tilt_term
+            up_acc[...] = up_term
+        else:
+            tilt_acc[...] += tilt_term
+            up_acc[...] += up_term
     g_norm[...] = tilt_acc[:8]
     g_up[...] = up_acc[:8]
-
-
-def call_qkv_back(ids, dq, dk, dv, w, normed, down, down_w, up_w):
+    wait_all(leave)
+
+
+def call_qkv_back(ids, dq, dk, dv, w, n_own, n_other, down, down_w, up_w):
     return pl.pallas_call(
         qkv_back_kernel,
         out_shape=(
@@ -848,12 +1028,22 @@
             shape(8, 1024, dtype=f32),
             shape(8, 1024, dtype=f32),
         ),
-        in_specs=[SMEM] + [VMEM] * 8,
-        out_specs=(VMEM,) * 4,
-        scratch_shapes=[pltpu.VMEM((128, 1024), f32), pltpu.VMEM((128, 1024), f32)],
-        compiler_params=params(40),
+        in_specs=[SMEM] + [HBM] * 7 + [VMEM] * 2,
+        out_specs=(HBM, HBM, VMEM, VMEM),
+        scratch_shapes=[pltpu.VMEM((4, BLOCK, HALF), bf16)] * 3
+        + [
+            pltpu.VMEM((3, 1024, HALF), bf16),
+            pltpu.VMEM((1024, 1024), bf16),
+            pltpu.VMEM((1024, 128), bf16),
+            pltpu.VMEM((HALF, 1024), bf16),
+            pltpu.VMEM((HALF, 1024), bf16),
+            pltpu.VMEM((128, 1024), f32),
+            pltpu.VMEM((128, 1024), f32),
+            pltpu.SemaphoreType.DMA((20,)),
+        ],
+        compiler_params=params(),
         name="qkv_back",
-    )(ids, dq, dk, dv, w, normed, down, down_w, up_w)
+    )(ids, dq, dk, dv, w, n_own, n_other, down, down_w, up_w)
 
 
 def input_grad_kernel(ids, x0, x1, own, other, grad_middle, gain, out0, out1):
@@ -862,7 +1052,7 @@
         tok = rows(parity(z, k), BLOCK)
         grad = own[tok].astype(f32) + other[tok].astype(f32)
         hat, inverse = center_scale(x[...].astype(f32))
-        out[...] = (grad_middle[tok] + norm_back(hat, inverse, grad * gain[...])).astype(bf16)
+        out[...] = (grad_middle[tok] + norm_back(hat, inverse, grad * gain[0:1])).astype(bf16)
 
 
 def call_input_grad(ids, x_own, own, other, grad_middle, gain):
@@ -871,7 +1061,7 @@
         out_shape=(shape(BLOCK, 1024),) * 2,
         in_specs=[SMEM] + [VMEM] * 6,
         out_specs=(VMEM,) * 2,
-        compiler_params=params(32),
+        compiler_params=params(),
         name="input_grad",
     )(ids, *x_own, own, other, grad_middle, gain)
 
@@ -897,13 +1087,22 @@
     return jnp.where(even, pair[0], pair[1]), jnp.where(even, pair[1], pair[0])
 
 
-def gather(shard):
-    by_x = lax.ppermute(shard, "x", SWAP)
-    by_y = lax.ppermute(shard, "y", SWAP)
-    half = shard.shape[0] // 2
-    top = lax.ppermute(by_x[:half], "y", SWAP)
-    low = lax.ppermute(by_y[half:], "x", SWAP)
-    return [shard, by_x, by_y, top, low]
+def after(value, *others):
+    return lax.optimization_barrier((value, *others))[0]
+
+
+def gather_near(shard):
+    return [shard, lax.ppermute(shard, "x", SWAP), lax.ppermute(shard, "y", SWAP)]
+
+
+def halves(near):
+    _, by_x, by_y = near
+    half = by_x.shape[0] // 2
+    return by_x[:half], by_y[half:]
+
+
+def gather_far(near, parts):
+    return near + [lax.ppermute(parts[0], "y", SWAP), lax.ppermute(parts[1], "x", SWAP)]
 
 
 def on_chip(
@@ -926,29 +1125,32 @@
     chip = 2 * lax.axis_index("y") + lax.axis_index("x")
     ids = jnp.stack([core, z, chip]).astype(jnp.int32)
 
-    by_core = qkv_weight.reshape(128, 12, 2, 128)
-    first, second = by_core[:, :, 0].reshape(128, 1536), by_core[:, :, 1].reshape(128, 1536)
-    kept = jnp.where(core == 0, first, second)
-    passed = jnp.where(core == 0, second, first)
-    got = to_core(passed)
-    qkv_shard = jnp.concatenate(
-        [jnp.where(core == 0, kept, got), jnp.where(core == 0, got, kept)], axis=0
-    )
-    x_own = exchange(z, by_parity(z, (inputs[0], inputs[1])))
-    x_other = [to_core(part) for part in x_own]
-    qkv_pieces = gather(qkv_shard)
-    out_pieces = gather(out_weight)
-    out_other = [to_core(part) for part in out_pieces]
-    in_pieces = gather(feed_input_weight)
-    in_other = [to_core(part) for part in in_pieces]
-    proj_pieces = gather(proj_weight)
-    proj_other = [to_core(part) for part in proj_pieces]
-    g_own = exchange(z, by_parity(z, (out_grad[0], out_grad[1])))
+    def choose(value, axis):
+        first, second = lax.index_in_dim(value, 0, axis, False), lax.index_in_dim(value, 1, axis, False)
+        return jnp.where(core == 0, first, second), jnp.where(core == 0, second, first)
+
+    qkv_own, qkv_send = choose(qkv_weight.reshape(128, 3, 4, 2, 128), 3)
+    qkv_own = qkv_own.transpose(1, 0, 2, 3).reshape(3, 128, HALF)
+    qkv_send = qkv_send.transpose(1, 0, 2, 3).reshape(3, 128, HALF)
+    qkv_got = to_core(qkv_send)
+    x_own = exchange(z, by_parity(z, after((inputs[0], inputs[1]), qkv_send)))
+    out_part = out_weight.reshape(128, 2, HALF).transpose(1, 0, 2).reshape(1, BLOCK, HALF)
+    first_shard = jnp.concatenate(
+        [jnp.concatenate([qkv_own, qkv_got], axis=1), after(out_part, qkv_send)], axis=0
+    )
+    first_near = gather_near(first_shard)
+    in_own, in_send = choose(after(feed_input_weight, first_shard).reshape(128, 4, 2, HALF), 2)
+    in_own, in_send = in_own.transpose(1, 0, 2), in_send.transpose(1, 0, 2)
+    in_shard = jnp.concatenate([in_own, to_core(in_send)], axis=1)
+    n_own = call_norm(ids, x_own, norm_gain, norm_bias)
+    n_other = to_core(n_own)
+    first_halves = halves(first_near)
+    first_pieces = gather_far(first_near, first_halves)
+    in_near = gather_near(after(in_shard, *first_halves))
 
     def columns(value):
         lead = value.shape[0]
-        value = value.reshape(lead, 4, 2, 128)
-        return jnp.where(core == 0, value[:, :, 0], value[:, :, 1]).reshape(lead, HALF)
+        return choose(value.reshape(lead, 4, 2, 128), 2)[0].reshape(lead, HALF)
 
     scale = adapter_alpha / ADAPTER_RANK
     up_q, up_v = scale * columns(adapters[1]), scale * columns(adapters[3])
@@ -959,40 +1161,46 @@
     head_bias = columns(proj_bias[:2])
     qkv_bias = jnp.concatenate([head_bias[0], jnp.zeros((HALF,), f32), head_bias[1]])[None]
 
-    q, k, v, normed, down, qkv_full = call_qkv(
-        ids, x_own, x_other, qkv_pieces, norm_gain[:1], norm_bias[:1], down_w, up_w, qkv_bias
-    )
-    ctx, stat, ctx_send = call_forward(ids, q, k, v)
-    ctx_other = to_core(ctx_send)
-    middle, normed_two, out_full = call_middle(
-        ids, ctx, ctx_other, out_pieces, out_other, x_own, proj_bias[2:3], norm_gain[1:], norm_bias[1:]
-    )
-    active, slope, w_in = call_hidden(ids, normed_two, in_pieces, in_other, fc_bias[None])
-    old = call_feed(
-        ids, ((0, 0), (0, 1)), g_own, active, slope, w_in, (proj_pieces[0], proj_other[0]), None
-    )
-    result, grad = call_feed(
-        ids,
-        ((1, 0), (1, 1), (2, 0), (2, 1)),
-        g_own,
-        active,
-        slope,
-        w_in,
-        (proj_pieces[1], proj_other[1], proj_pieces[2], proj_other[2]),
-        old,
-    )
-    halves = (proj_pieces[3], proj_pieces[4], proj_other[3], proj_other[4])
-    grad_middle, grad_ctx, grad_send = call_last_grad(
-        ids, g_own, slope, w_in, halves, grad, middle, norm_gain[1:], out_full
-    )
-    grad_ctx_other = to_core(grad_send)
-    mixed = exchange(z, call_last_result(ids, active, halves, result, middle, proj_bias[3:]))
-    dq, dk, dv = call_backward(ids, q, k, v, ctx, stat, grad_ctx, grad_ctx_other)
+    q, k, v, down, w_qkv, w_o = call_qkv(ids, n_own, n_other, first_pieces, down_w, up_w, qkv_bias)
+    g_own = exchange(z, after(by_parity(z, (out_grad[0], out_grad[1])), q))
+    ctx, stat, attn_own, attn_send = call_forward(ids, q, k, v, w_o)
+    attn_other = to_core(attn_send)
+    middle, n2_own = call_middle(
+        ids, attn_own, attn_other, x_own, proj_bias, norm_gain, norm_bias
+    )
+    n2_other = to_core(n2_own)
+    in_near = after(in_near, ctx)
+    in_halves = halves(in_near)
+    in_pieces = gather_far(in_near, in_halves)
+    proj_near = gather_near(after(proj_weight, *in_halves))
+    g_other = [to_core(part) for part in g_own]
+    active, slope, w_in = call_hidden(ids, n2_own, n2_other, in_pieces, fc_bias.reshape(8, HALF))
+    old = call_feed(ids, (0,), g_own, g_other, active, slope, w_in, proj_near[:1])
+    proj_near = after(proj_near, *old)
+    proj_halves = halves(proj_near)
+    far = gather_far(proj_near, proj_halves)[3:]
+    near = after(proj_near[1:], *proj_halves)
+    result, grad = call_feed(ids, (1, 2), g_own, g_other, active, slope, w_in, near, old)
+    grad_send = call_far_send(ids, g_other, slope, w_in, far, grad)
+    grad_other = to_core(grad_send)
+    result_own, result_send = call_far_result(ids, active, after(far, grad_send), result)
+    result_other = to_core(result_send)
+    grad_other = after(grad_other, result_own)
+    grad_middle, low_own = call_far_own(
+        ids, g_own, slope, w_in, far, grad, grad_other, middle, norm_gain
+    )
+    low_other = to_core(low_own)
+    mixed = call_mixed(ids, after(result_own, low_own), result_other, middle, proj_bias)
+    low_other = after(low_other, *mixed)
+    mixed = exchange(z, mixed)
+    dq, dk, dv = call_backward(ids, q, k, v, ctx, stat, w_o, low_own, low_other)
+    mixed = after(mixed, dq)
+    dq = after(dq, *mixed)
     own, send, g_norm, g_up = call_qkv_back(
-        ids, dq, dk, dv, qkv_full, normed, down, down_w, up_w
+        ids, dq, dk, dv, w_qkv, n_own, n_other, down, down_w, up_w
     )
     other = to_core(send)
-    grad_in = exchange(z, call_input_grad(ids, x_own, own, other, grad_middle, norm_gain[:1]))
+    grad_in = exchange(z, call_input_grad(ids, x_own, own, other, grad_middle, norm_gain))
 
     def spread(part):
         part = part.reshape(4, 4, 1, 128)

time: 353 us -> 292 us (0.83)
  waiting for transfers between devices: 134 us -> 68.5 us
  Pallas kernels: 111 us -> 140 us
  local copies, waits for them, and re-layouts: 43.5 us -> 22 us
  starting transfers between devices: 49.2 us -> 40.1 us
    ppermute x16 -> x12, waiting for transfers between devices: 67.8 us -> 9.91 us  [the longest x3 7.73 us: gather_far(): lax.ppermute(parts[0], 'y', SWAP)]
    unnamed x150 -> x37, local copies, waits for them, and re-layouts: 31.3 us -> 1.29 us
    pallas_call x5 -> x8, Pallas kernels: 55.3 us -> 64.5 us  [the longest x2 24.1 us: call_feed(): pl.pallas_call(functools.partial(feed_kernel, steps, not old), out_shape=...]
    pallas_call x1, Pallas kernels: 8.4 us -> 14.9 us  [call_qkv_back(): pl.pallas_call(qkv_back_kernel, out_shape=(shape(HALF, 1024), shape(HALF,...]
    ppermute x21 -> x11, starting transfers between devices: 11.4 us -> 5.22 us  [to_core(): return lax.ppermute(value, 'core', SWAP)]
    pallas_call x1, Pallas kernels: 18.2 us -> 23.1 us  [call_backward(): pl.pallas_call(backward_kernel, grid=(4,), out_shape=(shape(1024, HALF),)...]
    ppermute x21 -> x11, waiting for transfers between devices: 4.52 us -> 0.03 us  [to_core(): return lax.ppermute(value, 'core', SWAP)]
    reshape x1 -> x6, local copies, waits for them, and re-layouts: 0.02 us -> 4.26 us  [the longest x1 2.57 us: on_chip(): qkv_own, qkv_send = choose(qkv_weight.reshape(128, 3, 4, 2, 128), 3)]
  transfers between devices with their start and end apart: 50 -> 36, of which waited for: 21 -> 13; matrix products, arithmetic and copies ran while one was open for 6% -> 9% of each run, Pallas kernels for 21% -> 42%
where the time goes in v2:
time: 292 us; the launch traced here: 288 us
  Pallas kernels  140 us (48%)
  waiting for transfers between devices  68.5 us (23%)
  starting transfers between devices  40.1 us (14%)
  local copies, waits for them, and re-layouts  22 us (8%)
  other arithmetic  13.7 us (5%)
  between operations  3.31 us (1%)
    ppermute x8, waiting for transfers between devices, exchange(): sent.append(lax.ppermute(pair[k], ('core', 'seq'), perm))  50.3 us
    pallas_call x2, Pallas kernels, call_feed(): pl.pallas_call(functools.partial(feed_kernel, steps, not old), out_shape=...  24.1 us
    pallas_call x1, Pallas kernels, call_backward(): pl.pallas_call(backward_kernel, grid=(4,), out_shape=(shape(1024, HALF),)...  23.1 us
    ppermute x8, starting transfers between devices, exchange(): sent.append(lax.ppermute(pair[k], ('core', 'seq'), perm))  19.7 us
    pallas_call x1, Pallas kernels, call_forward(): pl.pallas_call(forward_kernel, grid=(4,), out_shape=(shape(1024, HALF), s...  17.6 us
    pallas_call x1, Pallas kernels, call_qkv_back(): pl.pallas_call(qkv_back_kernel, out_shape=(shape(HALF, 1024), shape(HALF,...  14.9 us
    pallas_call x1, Pallas kernels, call_hidden(): pl.pallas_call(hidden_kernel, out_shape=(shape(4, 1024, HALF),) * 3, in_s...  14.1 us
    pallas_call x1, Pallas kernels, call_qkv(): pl.pallas_call(qkv_kernel, out_shape=(shape(1024, HALF), shape(1024, HALF...  10.3 us
  transfers between devices with their start and end apart: 36, of which 13 were waited for; matrix products, arithmetic and copies ran while one was open for 9% of the time, Pallas kernels for 42%

profile of v2, /device:TPU:9, one launch (start us, length us, event | category | flops | bytes accessed | tf_op | source)
XLA Modules:
  0.0 287.5 jit_solution(7232997778650627447)
XLA Ops:
  0.6 2.6 reshape.225
  7.5 4.6 %collective-permute-start = (bf16[256,1024]{1,0:T(8,128)(2,1)}, bf16[256,1024]{1,0:T(8,128)(2,1)S(1)}, u32[]{:S(2)}, u32[]{:S(2)}) collective-permute-start(bf16[256,1024]{1,0:T(8,128)(2,1)} %get-tuple-element.164), channel_id=1, source_target_pairs={{0,0},{1,1},{2,4},{3,5},{4,2},{5,3},{6,6},{7,7},{8,8},{9,9},{10,12... | collective-permute-start | bytes 1572872 | tf_op jit(solution)/shard_map/ppermute | solution.py:1081
  13.8 2.0 pad_maximum_fusion.w0
  20.8 3.8 %collective-permute-done.m0.x0 = bf16[256,1024]{1,0:T(8,128)(2,1)S(1)} collective-permute-done((bf16[256,1024]{1,0:T(8,128)(2,1)}, bf16[256,1024]{1,0:T(8,128)(2,1)S(1)}, u32[]{:S(2)}, u32[]{:S(2)}) %collective-permute-start) | collective-permute-done | bytes 524320 | tf_op jit(solution)/shard_map/ppermute | solution.py:1081
  24.6 10.3 %collective-permute-done.1.m1.x1 = bf16[256,1024]{1,0:T(8,128)(2,1)} collective-permute-done((bf16[256,1024]{1,0:T(8,128)(2,1)}, bf16[256,1024]{1,0:T(8,128)(2,1)}, u32[]{:S(2)}, u32[]{:S(2)}) %collective-permute-start.1) | collective-permute-done | bytes 524320 | tf_op jit(solution)/shard_map/ppermute | solution.py:1081
  34.9 3.6 %norm.1.n_own = bf16[512,1024]{1,0:T(8,128)(2,1)} custom-call(s32[3]{0:T(128)} %pad_add_fusion.ids.refs_0_, bf16[256,1024]{1,0:T(8,128)(2,1)} %copy-done.2, bf16[256,1024]{1,0:T(8,128)(2,1)} %collective-permute-done.1.m1.x1, f32[2,1024]{1,0:T(2,128)} %gain.7, f32[2,1024]{1,0:T(2,128)} %shift.3), custom_call_target="tpu_custom_call" | custom-call | tf_op jit(solution)/shard_map/norm/pallas_call | solution.py:375
  49.1 7.7 %collective-permute-done.6.w3t = bf16[2,256,512]{2,1,0:T(8,128)(2,1)S(1)} collective-permute-done((bf16[2,256,512]{2,1,0:T(8,128)(2,1)S(1)}, bf16[2,256,512]{2,1,0:T(8,128)(2,1)S(1)}, u32[]{:S(2)}, u32[]{:S(2)}) %collective-permute-start.6) | collective-permute-done | bytes 524320 | tf_op jit(solution)/shard_map/ppermute | solution.py:1105
  56.8 2.2 collective-permute-done.7.w3b
  59.0 10.3 %qkv.1 = (bf16[1024,512]{1,0:T(8,128)(2,1)}, bf16[1024,512]{1,0:T(8,128)(2,1)}, bf16[1024,512]{1,0:T(8,128)(2,1)}, bf16[1024,128]{1,0:T(8,128)(2,1)}, bf16[3,102...) custom-call(s32[3]{0:T(128)} %pad_add_fusion.ids.refs_0_, bf16[512,1024]{1,0:T(8,128)(2,1)} %norm.1.n_own, ...), custom_call_target="tpu_custom_call" | custom-call | tf_op jit(solution)/shard_map/qkv/pallas_call | solution.py:438
  69.3 17.6 %attention.1 = (bf16[1024,512]{1,0:T(8,128)(2,1)}, f32[4,8,1024]{2,1,0:T(8,128)}, f32[512,1024]{1,0:T(8,128)}, bf16[512,1024]{1,0:T(8,128)(2,1)}) custom-call(s32[3]{0:T(128)} %pad_add_fusion.ids.refs_0_, bf16[1024,512]{1,0:T(8,128)(2,1)} %get-tuple-element.91.q, bf16[1024,512]{1,0:T(8,128)(2,1)} %get-tuple-element.92.k, ...), custom_call_target="tpu_custom_call" | custom-call | tf_op jit(solution)/shard_map/attention/pallas_call | solution.py:521
  88.9 2.2 select_bitcast_fusion.4
  91.2 2.1 collective-permute-start.17
  93.3 2.0 collective-permute-start.18
  97.4 4.5 %middle.1 = (f32[512,1024]{1,0:T(8,128)}, bf16[512,1024]{1,0:T(8,128)(2,1)}) custom-call(s32[3]{0:T(128)} %pad_add_fusion.ids.refs_0_, f32[512,1024]{1,0:T(8,128)} %get-tuple-element.95.own, bf16[512,1024]{1,0:T(8,128)(2,1)} %collective-permute-done.8.other, bf16[256,1024]{1,0:T(8,128)(2,1)} %copy-done.2, bf16[256,1024]{1,0:T(8,128)(2,1)} %collective-permute-done.1.m1.x1, ...), custom_call_target="tpu_custom_call" | custom-call | tf_op jit(solution)/shard_map/middle/pallas_call | solution.py:664
  104.3 3.7 %collective-permute-done.17.refs_1_.g0 = bf16[256,1024]{1,0:T(8,128)(2,1)S(1)} collective-permute-done((bf16[256,1024]{1,0:T(8,128)(2,1)}, bf16[256,1024]{1,0:T(8,128)(2,1)S(1)}, u32[]{:S(2)}, u32[]{:S(2)}) %collective-permute-start.17) | collective-permute-done | bytes 524320 | tf_op jit(solution)/shard_map/ppermute | solution.py:1081
  109.3 10.1 %collective-permute-done.18.refs_2_.g1 = bf16[256,1024]{1,0:T(8,128)(2,1)} collective-permute-done((bf16[256,1024]{1,0:T(8,128)(2,1)}, bf16[256,1024]{1,0:T(8,128)(2,1)}, u32[]{:S(2)}, u32[]{:S(2)}) %collective-permute-start.18) | collective-permute-done | bytes 524320 | tf_op jit(solution)/shard_map/ppermute | solution.py:1081
  120.7 14.1 %hidden.1 = (bf16[4,1024,512]{2,1,0:T(8,128)(2,1)}, bf16[4,1024,512]{2,1,0:T(8,128)(2,1)}, bf16[4,1024,512]{2,1,0:T(8,128)(2,1)}) custom-call(s32[3]{0:T(128)} %pad_add_fusion.ids.refs_0_, bf16[512,1024]{1,0:T(8,128)(2,1)} %get-tuple-element.97.n_own, bf16[512,1024]{1,0:T(8,128)(2,1)} %collective-permute-done.9.n_other, ...), custom_call_target="tpu_custom_call" | custom-call | tf_op jit(solution)/shard_map/hidden/pallas_call | solution.py:718
  134.8 9.2 %feed.2 = (f32[1024,1024]{1,0:T(8,128)}, f32[1024,1024]{1,0:T(8,128)}) custom-call(s32[3]{0:T(128)} %pad_add_fusion.ids.refs_0_, bf16[256,1024]{1,0:T(8,128)(2,1)} %copy-done, bf16[256,1024]{1,0:T(8,128)(2,1)} %collective-permute-done.18.refs_2_.g1, bf16[256,1024]{1,0:T(8,128)(2,1)} %collective-permute-done.19.refs_3_.g0, ...), custom_call_target="tpu_custom_call" | custom-call | tf_op jit(solution)/shard_map/feed/pallas_call | solution.py:796
  150.3 14.8 %feed.3 = (f32[1024,1024]{1,0:T(8,128)}, f32[1024,1024]{1,0:T(8,128)}) custom-call(s32[3]{0:T(128)} %pad_add_fusion.ids.refs_0_, bf16[256,1024]{1,0:T(8,128)(2,1)} %copy-done, bf16[256,1024]{1,0:T(8,128)(2,1)} %collective-permute-done.18.refs_2_.g1, bf16[256,1024]{1,0:T(8,128)(2,1)} %collective-permute-done.19.refs_3_.g0, ...), custom_call_target="tpu_custom_call" | custom-call | tf_op jit(solution)/shard_map/feed/pallas_call | solution.py:796
  166.0 5.4 %far_send.1 = bf16[512,1024]{1,0:T(8,128)(2,1)} custom-call(s32[3]{0:T(128)} %pad_add_fusion.ids.refs_0_, bf16[256,1024]{1,0:T(8,128)(2,1)} %collective-permute-done.19.refs_3_.g0, bf16[256,1024]{1,0:T(8,128)(2,1)} %collective-permute-done.20.refs_4_.g1, bf16[4,1024,512]{2,1,0:T(8,128)(2,1)} %get-tuple-element.108.refs_6_.slope, ...), custom_call_target="tpu_custom_call" | custom-call | tf_op jit(solution)/shard_map/far_send/pallas_call | solution.py:841
  172.1 5.9 %far_result.1 = (f32[512,1024]{1,0:T(8,128)}, bf16[512,1024]{1,0:T(8,128)(2,1)}) custom-call(s32[3]{0:T(128)} %pad_add_fusion.ids.refs_0_, bf16[4,1024,512]{2,1,0:T(8,128)(2,1)} %get-tuple-element.104.refs_5_.active, bf16[256,1024]{1,0:T(8,128)(2,1)} %copy-done.1, bf16[256,1024]{1,0:T(8,128)(2,1)} %collective-permute-done.22.low, ...), custom_call_target="tpu_custom_call" | custom-call | tf_op jit(solution)/shard_map/far_result/pallas_call | solution.py:941
  178.1 7.6 %far_own.1 = (f32[512,1024]{1,0:T(8,128)}, bf16[512,1024]{1,0:T(8,128)(2,1)}) custom-call(s32[3]{0:T(128)} %pad_add_fusion.ids.refs_0_, bf16[256,1024]{1,0:T(8,128)(2,1)} %copy-done, bf16[256,1024]{1,0:T(8,128)(2,1)} %collective-permute-done.18.refs_2_.g1, bf16[4,1024,512]{2,1,0:T(8,128)(2,1)} %get-tuple-element.108.refs_6_.slope, ...), custom_call_target="tpu_custom_call" | custom-call | tf_op jit(solution)/shard_map/far_own/pallas_call | solution.py:895
  186.2 3.8 %mixed.1 = (bf16[256,1024]{1,0:T(8,128)(2,1)}, bf16[256,1024]{1,0:T(8,128)(2,1)}) custom-call(s32[3]{0:T(128)} %pad_add_fusion.ids.refs_0_, f32[512,1024]{1,0:T(8,128)} %get-tuple-element.124.own, bf16[512,1024]{1,0:T(8,128)(2,1)} %collective-permute-done.24.other, f32[512,1024]{1,0:T(8,128)} %get-tuple-element.122.middle, f32[4,1024]{1,0:T(4,128)} %bias.3), custom_call_target="tpu_custom_call" | custom-call | tf_op jit(solution)/shard_map/mixed/pallas_call | solution.py:968
  190.0 3.5 %collective-permute-start.25 = (bf16[256,1024]{1,0:T(8,128)(2,1)}, bf16[256,1024]{1,0:T(8,128)(2,1)S(1)}, u32[]{:S(2)}, u32[]{:S(2)}) collective-permute-start(bf16[256,1024]{1,0:T(8,128)(2,1)} %get-tuple-element.126), channel_id=1, source_target_pairs={{0,0},{1,1},{2,4},{3,5},{4,2},{5,3},{6,6},{7,7},{8,8},{9,9},{10,12... | collective-permute-start | bytes 1572872 | tf_op jit(solution)/shard_map/ppermute | solution.py:1081
  193.8 23.1 %attention_back.1 = (bf16[1024,512]{1,0:T(8,128)(2,1)}, bf16[1024,512]{1,0:T(8,128)(2,1)}, bf16[1024,512]{1,0:T(8,128)(2,1)}) custom-call(s32[3]{0:T(128)} %pad_add_fusion.ids.refs_0_, bf16[1024,512]{1,0:T(8,128)(2,1)} %get-tuple-element.91.q, bf16[1024,512]{1,0:T(8,128)(2,1)} %get-tuple-element.92.k, bf16[1024,512]{1,0:T(8,128)(2,1)} %get-tuple-element.93.v, ...), custom_call_target="tpu_custom_call" | custom-call | tf_op jit(solution)/shard_map/attention_back/pallas_call | solution.py:608
  217.6 14.9 %qkv_back.1 = (bf16[512,1024]{1,0:T(8,128)(2,1)}, bf16[512,1024]{1,0:T(8,128)(2,1)}, f32[8,1024]{1,0:T(8,128)}, f32[8,1024]{1,0:T(8,128)}) custom-call(s32[3]{0:T(128)} %pad_add_fusion.ids.refs_0_, bf16[1024,512]{1,0:T(8,128)(2,1)} %get-tuple-element.133.dq, bf16[1024,512]{1,0:T(8,128)(2,1)} %get-tuple-element.134.dk, ...), custom_call_target="tpu_custom_call" | custom-call | tf_op jit(solution)/shard_map/qkv_back/pallas_call | solution.py:1023
  236.2 2.9 collective-permute-done.32
  239.4 2.9 %collective-permute-done.33 = f32[4,4,1024]{2,1,0:T(4,128)S(1)} collective-permute-done((f32[4,4,1024]{2,1,0:T(4,128)S(1)}, f32[4,4,1024]{2,1,0:T(4,128)S(1)}, u32[]{:S(2)}, u32[]{:S(2)}) %collective-permute-start.33) | collective-permute-done | bytes 65568 | tf_op jit(solution)/shard_map/ppermute | solution.py:1225
  246.9 5.0 %input_grad.1 = (bf16[256,1024]{1,0:T(8,128)(2,1)}, bf16[256,1024]{1,0:T(8,128)(2,1)}) custom-call(s32[3]{0:T(128)} %pad_add_fusion.ids.refs_0_, bf16[256,1024]{1,0:T(8,128)(2,1)} %copy-done.2, bf16[256,1024]{1,0:T(8,128)(2,1)} %collective-permute-done.1.m1.x1, bf16[512,1024]{1,0:T(8,128)(2,1)} %get-tuple-element.138.own, ...), custom_call_target="tpu_custom_call" | custom-call | tf_op jit(solution)/shard_map/input_grad/pallas_call | solution.py:1059
  251.8 6.9 %collective-permute-start.29 = (bf16[256,1024]{1,0:T(8,128)(2,1)}, bf16[256,1024]{1,0:T(8,128)(2,1)S(1)}, u32[]{:S(2)}, u32[]{:S(2)}) collective-permute-start(bf16[256,1024]{1,0:T(8,128)(2,1)} %get-tuple-element.141), channel_id=1, source_target_pairs={{0,0},{1,1},{2,4},{3,5},{4,2},{5,3},{6,6},{7,7},{8,8},{9,9},{10,12... | collective-permute-start | bytes 1572872 | tf_op jit(solution)/shard_map/ppermute | solution.py:1081
  261.3 8.2 %collective-permute-done.29 = bf16[256,1024]{1,0:T(8,128)(2,1)S(1)} collective-permute-done((bf16[256,1024]{1,0:T(8,128)(2,1)}, bf16[256,1024]{1,0:T(8,128)(2,1)S(1)}, u32[]{:S(2)}, u32[]{:S(2)}) %collective-permute-start.29) | collective-permute-done | bytes 524320 | tf_op jit(solution)/shard_map/ppermute | solution.py:1081
  269.6 13.3 %collective-permute-done.30 = bf16[256,1024]{1,0:T(8,128)(2,1)S(1)} collective-permute-done((bf16[256,1024]{1,0:T(8,128)(2,1)}, bf16[256,1024]{1,0:T(8,128)(2,1)S(1)}, u32[]{:S(2)}, u32[]{:S(2)}) %collective-permute-start.30) | collective-permute-done | bytes 524320 | tf_op jit(solution)/shard_map/ppermute | solution.py:1081
  (157 shorter events, 53.2 us)
Async XLA Ops:
  5.6 8.1 %collective-permute-start.3 = (bf16[3,128,512]{2,1,0:T(8,128)(2,1)}, bf16[3,128,512]{2,1,0:T(8,128)(2,1)}, u32[]{:S(2)}, u32[]{:S(2)}) collective-permute-start(bf16[3,128,512]{2,1,0:T(8,128)(2,1)} %reshape.226), channel_id=1, source_target_pairs={{0,4},{4,0},{1,5},{5,1},{2,6},{6,2},{3,7},{7,3},{8,12},{12,8},{9,1... | collective-permute-start | bytes 1179656 | tf_op jit(solution)/shard_map/ppermute | solution.py:1070
  7.5 17.2 %collective-permute-start = (bf16[256,1024]{1,0:T(8,128)(2,1)}, bf16[256,1024]{1,0:T(8,128)(2,1)S(1)}, u32[]{:S(2)}, u32[]{:S(2)}) collective-permute-start(bf16[256,1024]{1,0:T(8,128)(2,1)} %get-tuple-element.164), channel_id=1, source_target_pairs={{0,0},{1,1},{2,4},{3,5},{4,2},{5,3},{6,6},{7,7},{8,8},{9,9},{10,12... | collective-permute-start | bytes 1572872 | tf_op jit(solution)/shard_map/ppermute | solution.py:1081
  12.0 22.9 %collective-permute-start.1 = (bf16[256,1024]{1,0:T(8,128)(2,1)}, bf16[256,1024]{1,0:T(8,128)(2,1)}, u32[]{:S(2)}, u32[]{:S(2)}) collective-permute-start(bf16[256,1024]{1,0:T(8,128)(2,1)} %get-tuple-element.163), channel_id=1, source_target_pairs={{0,1},{1,0},{2,5},{3,4},{4,3},{5,2},{6,7},{7,6},{8,9},{9,8},{10,13... | collective-permute-start | bytes 1572872 | tf_op jit(solution)/shard_map/ppermute | solution.py:1081
  15.8 25.9 %collective-permute-start.4 = (bf16[4,256,512]{2,1,0:T(8,128)(2,1)}, bf16[4,256,512]{2,1,0:T(8,128)(2,1)}, u32[]{:S(2)}, u32[]{:S(2)}) collective-permute-start(bf16[4,256,512]{2,1,0:T(8,128)(2,1)} %pad_maximum_fusion.w0), channel_id=1, source_target_pairs={{0,8},{8,0},{1,9},{9,1},{2,10},{10,2},{3,11},{11,3},{4,12},{12,4},... | collective-permute-start | bytes 3145736 | tf_op jit(solution)/shard_map/ppermute | solution.py:1095
  17.0 27.5 %collective-permute-start.5 = (bf16[4,256,512]{2,1,0:T(8,128)(2,1)}, bf16[4,256,512]{2,1,0:T(8,128)(2,1)}, u32[]{:S(2)}, u32[]{:S(2)}) collective-permute-start(bf16[4,256,512]{2,1,0:T(8,128)(2,1)} %pad_maximum_fusion.w0), channel_id=1, source_target_pairs={{0,16},{16,0},{1,17},{17,1},{2,18},{18,2},{3,19},{19,3},{4,20},{20... | collective-permute-start | bytes 3145736 | tf_op jit(solution)/shard_map/ppermute | solution.py:1095
  38.5 10.6 %collective-permute-start.2 = (bf16[512,1024]{1,0:T(8,128)(2,1)}, bf16[512,1024]{1,0:T(8,128)(2,1)}, u32[]{:S(2)}, u32[]{:S(2)}) collective-permute-start(bf16[512,1024]{1,0:T(8,128)(2,1)} %norm.1.n_own), channel_id=1, source_target_pairs={{0,4},{4,0},{1,5},{5,1},{2,6},{6,2},{3,7},{7,3},{8,12},{12,8},{9,1... | collective-permute-start | bytes 3145736 | tf_op jit(solution)/shard_map/ppermute | solution.py:1070
  40.5 7.3 %collective-permute-start.10 = (bf16[4,128,512]{2,1,0:T(8,128)(2,1)S(1)}, bf16[4,128,512]{2,1,0:T(8,128)(2,1)S(1)}, u32[]{:S(2)}, u32[]{:S(2)}) collective-permute-start(bf16[4,128,512]{2,1,0:T(8,128)(2,1)S(1)} %get-tuple-element.160), channel_id=1, source_target_pairs={{0,4},{4,0},{1,5},{5,1},{2,6},{6,2},{3,7},{7,3},{8,12},{12,8},{9,1... | collective-permute-start | bytes 1572872 | tf_op jit(solution)/shard_map/ppermute | solution.py:1070
  42.8 14.0 %collective-permute-start.6 = (bf16[2,256,512]{2,1,0:T(8,128)(2,1)S(1)}, bf16[2,256,512]{2,1,0:T(8,128)(2,1)S(1)}, u32[]{:S(2)}, u32[]{:S(2)}) collective-permute-start(bf16[2,256,512]{2,1,0:T(8,128)(2,1)S(1)} %slice.175), channel_id=1, source_target_pairs={{0,16},{16,0},{1,17},{17,1},{2,18},{18,2},{3,19},{19,3},{4,20},{20... | collective-permute-start | bytes 1572872 | tf_op jit(solution)/shard_map/ppermute | solution.py:1105
  45.6 13.4 %collective-permute-start.7 = (bf16[2,256,512]{2,1,0:T(8,128)(2,1)S(1)}, bf16[2,256,512]{2,1,0:T(8,128)(2,1)}, u32[]{:S(2)}, u32[]{:S(2)}) collective-permute-start(bf16[2,256,512]{2,1,0:T(8,128)(2,1)S(1)} %slice.176), channel_id=1, source_target_pairs={{0,8},{8,0},{1,9},{9,1},{2,10},{10,2},{3,11},{11,3},{4,12},{12,4},... | collective-permute-start | bytes 1572872 | tf_op jit(solution)/shard_map/ppermute | solution.py:1105
  48.8 46.5 %collective-permute-start.11 = (bf16[4,256,512]{2,1,0:T(8,128)(2,1)}, bf16[4,256,512]{2,1,0:T(8,128)(2,1)}, u32[]{:S(2)}, u32[]{:S(2)}) collective-permute-start(bf16[4,256,512]{2,1,0:T(8,128)(2,1)} %pad_maximum_fusion.1.w0), channel_id=1, source_target_pairs={{0,8},{8,0},{1,9},{9,1},{2,10},{10,2},{3,11},{11,3},{4,12},{12,4},... | collective-permute-start | bytes 3145736 | tf_op jit(solution)/shard_map/ppermute | solution.py:1095
  49.1 46.2 %collective-permute-start.12 = (bf16[4,256,512]{2,1,0:T(8,128)(2,1)}, bf16[4,256,512]{2,1,0:T(8,128)(2,1)}, u32[]{:S(2)}, u32[]{:S(2)}) collective-permute-start(bf16[4,256,512]{2,1,0:T(8,128)(2,1)} %pad_maximum_fusion.1.w0), channel_id=1, source_target_pairs={{0,16},{16,0},{1,17},{17,1},{2,18},{18,2},{3,19},{19,3},{4,20},{20... | collective-permute-start | bytes 3145736 | tf_op jit(solution)/shard_map/ppermute | solution.py:1095
  87.0 10.4 %collective-permute-start.8 = (bf16[512,1024]{1,0:T(8,128)(2,1)}, bf16[512,1024]{1,0:T(8,128)(2,1)}, u32[]{:S(2)}, u32[]{:S(2)}) collective-permute-start(bf16[512,1024]{1,0:T(8,128)(2,1)} %get-tuple-element.96), channel_id=1, source_target_pairs={{0,4},{4,0},{1,5},{5,1},{2,6},{6,2},{3,7},{7,3},{8,12},{12,8},{9,1... | collective-permute-start | bytes 3145736 | tf_op jit(solution)/shard_map/ppermute | solution.py:1070
  91.2 16.9 %collective-permute-start.17 = (bf16[256,1024]{1,0:T(8,128)(2,1)}, bf16[256,1024]{1,0:T(8,128)(2,1)S(1)}, u32[]{:S(2)}, u32[]{:S(2)}) collective-permute-start(bf16[256,1024]{1,0:T(8,128)(2,1)} %get-tuple-element.106), channel_id=1, source_target_pairs={{0,0},{1,1},{2,4},{3,5},{4,2},{5,3},{6,6},{7,7},{8,8},{9,9},{10,12... | collective-permute-start | bytes 1572872 | tf_op jit(solution)/shard_map/ppermute | solution.py:1081
  93.3 26.1 %collective-permute-start.18 = (bf16[256,1024]{1,0:T(8,128)(2,1)}, bf16[256,1024]{1,0:T(8,128)(2,1)}, u32[]{:S(2)}, u32[]{:S(2)}) collective-permute-start(bf16[256,1024]{1,0:T(8,128)(2,1)} %get-tuple-element.107), channel_id=1, source_target_pairs={{0,1},{1,0},{2,5},{3,4},{4,3},{5,2},{6,7},{7,6},{8,9},{9,8},{10,13... | collective-permute-start | bytes 1572872 | tf_op jit(solution)/shard_map/ppermute | solution.py:1081
  97.2 22.4 %collective-permute-start.13 = (bf16[2,256,512]{2,1,0:T(8,128)(2,1)}, bf16[2,256,512]{2,1,0:T(8,128)(2,1)}, u32[]{:S(2)}, u32[]{:S(2)}) collective-permute-start(bf16[2,256,512]{2,1,0:T(8,128)(2,1)} %slice.163), channel_id=1, source_target_pairs={{0,16},{16,0},{1,17},{17,1},{2,18},{18,2},{3,19},{19,3},{4,20},{20... | collective-permute-start | bytes 1572872 | tf_op jit(solution)/shard_map/ppermute | solution.py:1105
  101.9 18.8 %collective-permute-start.9 = (bf16[512,1024]{1,0:T(8,128)(2,1)}, bf16[512,1024]{1,0:T(8,128)(2,1)}, u32[]{:S(2)}, u32[]{:S(2)}) collective-permute-start(bf16[512,1024]{1,0:T(8,128)(2,1)} %get-tuple-element.97.n_own), channel_id=1, source_target_pairs={{0,4},{4,0},{1,5},{5,1},{2,6},{6,2},{3,7},{7,3},{8,12},{12,8},{9,1... | collective-permute-start | bytes 3145736 | tf_op jit(solution)/shard_map/ppermute | solution.py:1070
  103.0 16.6 %collective-permute-start.14 = (bf16[2,256,512]{2,1,0:T(8,128)(2,1)S(1)}, bf16[2,256,512]{2,1,0:T(8,128)(2,1)}, u32[]{:S(2)}, u32[]{:S(2)}) collective-permute-start(bf16[2,256,512]{2,1,0:T(8,128)(2,1)S(1)} %slice.164), channel_id=1, source_target_pairs={{0,8},{8,0},{1,9},{9,1},{2,10},{10,2},{3,11},{11,3},{4,12},{12,4},... | collective-permute-start | bytes 1572872 | tf_op jit(solution)/shard_map/ppermute | solution.py:1105
  108.1 36.0 %collective-permute-start.15 = (bf16[512,1024]{1,0:T(8,128)(2,1)}, bf16[512,1024]{1,0:T(8,128)(2,1)}, u32[]{:S(2)}, u32[]{:S(2)}) collective-permute-start(bf16[512,1024]{1,0:T(8,128)(2,1)} %refs_8_), channel_id=1, source_target_pairs={{0,8},{8,0},{1,9},{9,1},{2,10},{10,2},{3,11},{11,3},{4,12},{12,4},... | collective-permute-start | bytes 3145736 | tf_op jit(solution)/shard_map/ppermute | solution.py:1095
  119.4 24.7 %collective-permute-start.16 = (bf16[512,1024]{1,0:T(8,128)(2,1)}, bf16[512,1024]{1,0:T(8,128)(2,1)}, u32[]{:S(2)}, u32[]{:S(2)}) collective-permute-start(bf16[512,1024]{1,0:T(8,128)(2,1)} %refs_8_), channel_id=1, source_target_pairs={{0,16},{16,0},{1,17},{17,1},{2,18},{18,2},{3,19},{19,3},{4,20},{20... | collective-permute-start | bytes 3145736 | tf_op jit(solution)/shard_map/ppermute | solution.py:1095
  119.6 15.2 %collective-permute-start.19 = (bf16[256,1024]{1,0:T(8,128)(2,1)S(1)}, bf16[256,1024]{1,0:T(8,128)(2,1)}, u32[]{:S(2)}, u32[]{:S(2)}) collective-permute-start(bf16[256,1024]{1,0:T(8,128)(2,1)S(1)} %collective-permute-done.17.refs_1_.g0), channel_id=1, source_target_pairs={{0,4},{4,0},{1,5},{5,1},{2,6},{6,2},{3,7},{7,3},{8,12},{12,8},{9,1... | collective-permute-start | bytes 1572872 | tf_op jit(solution)/shard_map/ppermute | solution.py:1070
  119.6 15.2 %collective-permute-start.20 = (bf16[256,1024]{1,0:T(8,128)(2,1)}, bf16[256,1024]{1,0:T(8,128)(2,1)}, u32[]{:S(2)}, u32[]{:S(2)}) collective-permute-start(bf16[256,1024]{1,0:T(8,128)(2,1)} %collective-permute-done.18.refs_2_.g1), channel_id=1, source_target_pairs={{0,4},{4,0},{1,5},{5,1},{2,6},{6,2},{3,7},{7,3},{8,12},{12,8},{9,1... | collective-permute-start | bytes 1572872 | tf_op jit(solution)/shard_map/ppermute | solution.py:1070
  146.0 19.2 %collective-permute-start.21 = (bf16[256,1024]{1,0:T(8,128)(2,1)}, bf16[256,1024]{1,0:T(8,128)(2,1)S(1)}, u32[]{:S(2)}, u32[]{:S(2)}) collective-permute-start(bf16[256,1024]{1,0:T(8,128)(2,1)} %slice.167), channel_id=1, source_target_pairs={{0,16},{16,0},{1,17},{17,1},{2,18},{18,2},{3,19},{19,3},{4,20},{20... | collective-permute-start | bytes 1572872 | tf_op jit(solution)/shard_map/ppermute | solution.py:1105
  149.1 16.1 %collective-permute-start.22 = (bf16[256,1024]{1,0:T(8,128)(2,1)}, bf16[256,1024]{1,0:T(8,128)(2,1)}, u32[]{:S(2)}, u32[]{:S(2)}) collective-permute-start(bf16[256,1024]{1,0:T(8,128)(2,1)} %slice.168), channel_id=1, source_target_pairs={{0,8},{8,0},{1,9},{9,1},{2,10},{10,2},{3,11},{11,3},{4,12},{12,4},... | collective-permute-start | bytes 1572872 | tf_op jit(solution)/shard_map/ppermute | solution.py:1105
  171.4 6.7 %collective-permute-start.23 = (bf16[512,1024]{1,0:T(8,128)(2,1)}, bf16[512,1024]{1,0:T(8,128)(2,1)}, u32[]{:S(2)}, u32[]{:S(2)}) collective-permute-start(bf16[512,1024]{1,0:T(8,128)(2,1)} %far_send.1), channel_id=1, source_target_pairs={{0,4},{4,0},{1,5},{5,1},{2,6},{6,2},{3,7},{7,3},{8,12},{12,8},{9,1... | collective-permute-start | bytes 3145736 | tf_op jit(solution)/shard_map/ppermute | solution.py:1070
  178.0 8.2 %collective-permute-start.24 = (bf16[512,1024]{1,0:T(8,128)(2,1)}, bf16[512,1024]{1,0:T(8,128)(2,1)}, u32[]{:S(2)}, u32[]{:S(2)}) collective-permute-start(bf16[512,1024]{1,0:T(8,128)(2,1)} %get-tuple-element.125), channel_id=1, source_target_pairs={{0,4},{4,0},{1,5},{5,1},{2,6},{6,2},{3,7},{7,3},{8,12},{12,8},{9,1... | collective-permute-start | bytes 3145736 | tf_op jit(solution)/shard_map/ppermute | solution.py:1070
  185.7 8.1 %collective-permute-start.27 = (bf16[512,1024]{1,0:T(8,128)(2,1)}, bf16[512,1024]{1,0:T(8,128)(2,1)}, u32[]{:S(2)}, u32[]{:S(2)}) collective-permute-start(bf16[512,1024]{1,0:T(8,128)(2,1)} %get-tuple-element.123.g_own), channel_id=1, source_target_pairs={{0,4},{4,0},{1,5},{5,1},{2,6},{6,2},{3,7},{7,3},{8,12},{12,8},{9,1... | collective-permute-start | bytes 3145736 | tf_op jit(solution)/shard_map/ppermute | solution.py:1070
  190.0 26.8 %collective-permute-start.25 = (bf16[256,1024]{1,0:T(8,128)(2,1)}, bf16[256,1024]{1,0:T(8,128)(2,1)S(1)}, u32[]{:S(2)}, u32[]{:S(2)}) collective-permute-start(bf16[256,1024]{1,0:T(8,128)(2,1)} %get-tuple-element.126), channel_id=1, source_target_pairs={{0,0},{1,1},{2,4},{3,5},{4,2},{5,3},{6,6},{7,7},{8,8},{9,9},{10,12... | collective-permute-start | bytes 1572872 | tf_op jit(solution)/shard_map/ppermute | solution.py:1081
  193.6 24.1 %collective-permute-start.26 = (bf16[256,1024]{1,0:T(8,128)(2,1)}, bf16[256,1024]{1,0:T(8,128)(2,1)}, u32[]{:S(2)}, u32[]{:S(2)}) collective-permute-start(bf16[256,1024]{1,0:T(8,128)(2,1)} %get-tuple-element.127), channel_id=1, source_target_pairs={{0,1},{1,0},{2,5},{3,4},{4,3},{5,2},{6,7},{7,6},{8,9},{9,8},{10,13... | collective-permute-start | bytes 1572872 | tf_op jit(solution)/shard_map/ppermute | solution.py:1081
  232.6 14.3 %collective-permute-start.28 = (bf16[512,1024]{1,0:T(8,128)(2,1)}, bf16[512,1024]{1,0:T(8,128)(2,1)}, u32[]{:S(2)}, u32[]{:S(2)}) collective-permute-start(bf16[512,1024]{1,0:T(8,128)(2,1)} %get-tuple-element.139), channel_id=1, source_target_pairs={{0,4},{4,0},{1,5},{5,1},{2,6},{6,2},{3,7},{7,3},{8,12},{12,8},{9,1... | collective-permute-start | bytes 3145736 | tf_op jit(solution)/shard_map/ppermute | solution.py:1070
  245.5 13.6 %collective-permute-start.35 = (f32[4,4,1024]{2,1,0:T(4,128)S(1)}, f32[4,4,1024]{2,1,0:T(4,128)S(1)}, u32[]{:S(2)}, u32[]{:S(2)}) collective-permute-start(f32[4,4,1024]{2,1,0:T(4,128)S(1)} %add.43), channel_id=1, source_target_pairs={{0,2},{2,0},{1,3},{3,1},{4,6},{6,4},{5,7},{7,5},{8,10},{10,8},{9,1... | collective-permute-start | bytes 196616 | tf_op jit(solution)/shard_map/ppermute | solution.py:1225
  251.8 17.7 %collective-permute-start.29 = (bf16[256,1024]{1,0:T(8,128)(2,1)}, bf16[256,1024]{1,0:T(8,128)(2,1)S(1)}, u32[]{:S(2)}, u32[]{:S(2)}) collective-permute-start(bf16[256,1024]{1,0:T(8,128)(2,1)} %get-tuple-element.141), channel_id=1, source_target_pairs={{0,0},{1,1},{2,4},{3,5},{4,2},{5,3},{6,6},{7,7},{8,8},{9,9},{10,12... | collective-permute-start | bytes 1572872 | tf_op jit(solution)/shard_map/ppermute | solution.py:1081
  258.8 24.1 %collective-permute-start.30 = (bf16[256,1024]{1,0:T(8,128)(2,1)}, bf16[256,1024]{1,0:T(8,128)(2,1)S(1)}, u32[]{:S(2)}, u32[]{:S(2)}) collective-permute-start(bf16[256,1024]{1,0:T(8,128)(2,1)} %get-tuple-element.142), channel_id=1, source_target_pairs={{0,1},{1,0},{2,5},{3,4},{4,3},{5,2},{6,7},{7,6},{8,9},{9,8},{10,13... | collective-permute-start | bytes 1572872 | tf_op jit(solution)/shard_map/ppermute | solution.py:1081
  (22 other events, 162.1 us)
